TPU v7x, 128 devices: a whole 4x4x4 slice. The times are simulated.
128 devices in a mesh: dom: 64 (over y, x, z), rep: 2 (over core).
Axes of the slice: x: 4, y: 4, z: 4, core: 2. Of those that a mesh axis runs over, the one named last changes fastest.
Arguments:
- node_state: bfloat16 [32768, 384], P(('rep', 'dom')), parts along dimension 0, may hold values from -6 to 6
- edge_state: bfloat16 [131072, 384], P(('rep', 'dom')), parts along dimension 0, may hold values from -6 to 6
- edge_source: int32 [131072], P(('rep', 'dom')), parts along dimension 0, may hold values from 0 to 383
- contact_block: int32 [2048], P(('rep', 'dom')), parts along dimension 0, may hold values from 0 to 1
- contact_host: int32 [2048, 1], P(('rep', 'dom')), parts along dimension 0, may hold values from 0 to 63; in each aligned block of 16 rows (0 to 15, 16 to 31, ...) at most 2 rows name the same one
- contact_remote: int32 [2048], P(('rep', 'dom')), parts along dimension 0, may hold values from 0 to 1
- w_edge_in: bfloat16 [2304, 384], P('rep'), parts along dimension 0, may hold values from -0.1875 to 0.1875
- w_edge_out: bfloat16 [768, 384], P('rep'), parts along dimension 0, may hold values from -0.3125 to 0.3125
- w_node_in: bfloat16 [2304, 384], P('rep'), parts along dimension 0, may hold values from -0.1875 to 0.1875
- w_node_out: bfloat16 [768, 384], P('rep'), parts along dimension 0, may hold values from -0.3125 to 0.3125
- w_contact_in: bfloat16 [1536, 384], P('rep'), parts along dimension 0, may hold values from -0.21875 to 0.21875
- w_contact_out: bfloat16 [768, 384], P('rep'), parts along dimension 0, may hold values from -0.3125 to 0.3125
- node_cot: bfloat16 [32768, 384], P(('rep', 'dom')), parts along dimension 0, may hold values from -6 to 6
- edge_cot: bfloat16 [131072, 384], P(('rep', 'dom')), parts along dimension 0, may hold values from -6 to 6
Outputs:
- node_out: bfloat16 [32768, 384], P(('rep', 'dom')), parts along dimension 0
- edge_out: bfloat16 [131072, 384], P(('rep', 'dom')), parts along dimension 0
- node_grad: bfloat16 [32768, 384], P(('rep', 'dom')), parts along dimension 0
- edge_grad: bfloat16 [131072, 384], P(('rep', 'dom')), parts along dimension 0
- grad_edge_in: float32 [2304, 384], P('rep'), parts along dimension 0
- grad_edge_out: float32 [768, 384], P('rep'), parts along dimension 0
- grad_node_in: float32 [2304, 384], P('rep'), parts along dimension 0
- grad_node_out: float32 [768, 384], P('rep'), parts along dimension 0
- grad_contact_in: float32 [1536, 384], P('rep'), parts along dimension 0
- grad_contact_out: float32 [768, 384], P('rep'), parts along dimension 0
There are 2 independent parts, one for each index of `rep`. A program takes and returns all parts, laid end to end along the dimension named above; each array names one. Nothing has to cross between parts.
Inputs may be any that keep to these rules, and one draw needn't show every extreme that they name: `contact_host`: the 16 rows of one partition name any one host partition at most 2 times, and 2 times in some partition.
All inputs are finite; a program needn't handle non-finite values.
Results may differ from a plain program's by a relative error of at most 0.0082.
Values may be sent and summed in bfloat16 or wider, within the bound.
A program may use at most 128 MiB of HBM per device.

v0:
```python
import jax
import jax.numpy as jnp
from jax import lax
from jax.sharding import PartitionSpec as P

BLOCK = 128
EPN = 4
RIM = 64
CAP = 2


norm_eps = 1e-05


def with_halo(value, sides, width):
    for axis, dim in sides:
        peers, length = (lax.axis_size(axis), value.shape[dim])
        up = [(i, (i + 1) % peers) for i in range(peers - 1)]
        down = [(j, i) for i, j in up]
        last = lax.slice_in_dim(value, length - width, length, axis=dim)
        initial = lax.slice_in_dim(value, 0, width, axis=dim)
        before = lax.ppermute(last, axis, up)
        after = lax.ppermute(initial, axis, down)
        value = jnp.concatenate([before, value, after], axis=dim)
    return value


def layer_norm(values):
    center = values - jnp.mean(values, axis=-1, keepdims=True)
    scale = lax.rsqrt(jnp.mean(center * center, axis=-1, keepdims=True) + norm_eps)
    return center * scale


def layer_norm_back(values, upstream):
    center = values - jnp.mean(values, axis=-1, keepdims=True)
    scale = lax.rsqrt(jnp.mean(center * center, axis=-1, keepdims=True) + norm_eps)
    normed = center * scale
    first = jnp.mean(upstream, axis=-1, keepdims=True)
    second = jnp.mean(upstream * normed, axis=-1, keepdims=True)
    return scale * (upstream - first - normed * second)


def forward_mlp(inputs, w_first, w_second):
    hidden_pre = jnp.dot(inputs, w_first, preferred_element_type=jnp.float32)
    hidden = jax.nn.silu(hidden_pre).astype(jnp.bfloat16)
    linear = jnp.dot(hidden, w_second, preferred_element_type=jnp.float32)
    return (hidden_pre, hidden, linear, layer_norm(linear))


def backward_mlp(inputs, hidden_pre, hidden, linear, w_second, upstream):
    d_linear = layer_norm_back(linear, upstream).astype(jnp.bfloat16)
    grad_second = jnp.dot(hidden.T, d_linear, preferred_element_type=jnp.float32)
    d_hidden = jnp.dot(d_linear, w_second.T, preferred_element_type=jnp.float32)
    sigma = jax.nn.sigmoid(hidden_pre)
    d_pre = (d_hidden * sigma * (1.0 + hidden_pre * (1.0 - sigma))).astype(jnp.bfloat16)
    grad_first = jnp.dot(inputs.T, d_pre, preferred_element_type=jnp.float32)
    return (d_pre, grad_first, grad_second)


def on_device(
    node_state,
    edge_state,
    edge_source,
    contact_block,
    contact_host,
    contact_remote,
    w_edge_in,
    w_edge_out,
    w_node_in,
    w_node_out,
    w_contact_in,
    w_contact_out,
    node_cot,
    edge_cot,
):
    node_count = node_state.shape[0]
    latent = node_state.shape[1]
    groups = lax.axis_size("dom")
    blocks = node_count // BLOCK
    slot_count = groups * CAP
    row_count = contact_block.shape[0]
    extended = with_halo(node_state, (("dom", 0),), RIM)
    source_rows = extended[edge_source]
    target_rows = jnp.repeat(node_state, EPN, axis=0)
    edge_input = jnp.concatenate([edge_state, source_rows, target_rows], axis=1)
    e_pre, e_hidden, e_linear, e_normed = forward_mlp(edge_input, w_edge_in, w_edge_out)
    edge_out = (edge_state.astype(jnp.float32) + e_normed).astype(jnp.bfloat16)
    mesh_sum = (
        edge_out.astype(jnp.float32)
        .reshape(node_count, EPN, latent)
        .sum(axis=1)
        .astype(jnp.bfloat16)
    )
    host_part = contact_host[:, 0]
    peer_ids = lax.iota(jnp.int32, groups)
    to_peer = (host_part[:, None] == peer_ids[None, :]).astype(jnp.int32)
    slot_rank = jnp.sum((jnp.cumsum(to_peer, axis=0) - to_peer) * to_peer, axis=1)
    slot_index = host_part * CAP + slot_rank
    slot_hit = slot_index[None, :] == lax.iota(jnp.int32, slot_count)[:, None]
    wanted = jnp.sum(slot_hit.astype(jnp.int32) * (contact_remote[None, :] + 1), axis=1).reshape(
        groups, CAP
    )
    asked_ids = lax.all_to_all(wanted, "dom", split_axis=0, concat_axis=0, tiled=True).reshape(
        slot_count
    )
    asked_block = jnp.maximum(asked_ids - 1, 0)
    asked_live = asked_ids > 0
    block_rows = node_state.reshape(blocks, BLOCK * latent)
    reply_rows = jnp.where(
        asked_live[:, None], block_rows[asked_block], jnp.zeros((), jnp.bfloat16)
    )
    arrived = lax.all_to_all(
        reply_rows.reshape(groups, CAP, BLOCK * latent),
        "dom",
        split_axis=0,
        concat_axis=0,
        tiled=True,
    )
    remote_rows = arrived.reshape(slot_count, BLOCK * latent)[slot_index].reshape(
        row_count * BLOCK, latent
    )
    own_rows = block_rows[contact_block].reshape(row_count * BLOCK, latent)
    contact_input = jnp.concatenate([own_rows, remote_rows], axis=1)
    c_pre, c_hidden, c_linear, c_normed = forward_mlp(contact_input, w_contact_in, w_contact_out)
    message = c_normed.astype(jnp.bfloat16)
    block_hit = contact_block[None, :] == lax.iota(jnp.int32, blocks)[:, None]
    contact_sum = jnp.dot(
        block_hit.astype(jnp.bfloat16),
        message.reshape(row_count, BLOCK * latent),
        preferred_element_type=jnp.float32,
    )
    contact_sum = contact_sum.reshape(node_count, latent).astype(jnp.bfloat16)
    node_input = jnp.concatenate([node_state, mesh_sum, contact_sum], axis=1)
    n_pre, n_hidden, n_linear, n_normed = forward_mlp(node_input, w_node_in, w_node_out)
    node_out = (node_state.astype(jnp.float32) + n_normed).astype(jnp.bfloat16)
    d_node_pre, grad_node_in, grad_node_out = backward_mlp(
        node_input, n_pre, n_hidden, n_linear, w_node_out, node_cot.astype(jnp.float32)
    )
    dx_node = jnp.dot(d_node_pre, w_node_in.T, preferred_element_type=jnp.float32)
    grad_h = node_cot.astype(jnp.float32) + dx_node[:, :latent]
    d_mesh = dx_node[:, latent : 2 * latent].astype(jnp.bfloat16)
    d_contact = dx_node[:, 2 * latent :].astype(jnp.bfloat16)
    d_edge = edge_cot.astype(jnp.float32) + jnp.repeat(d_mesh.astype(jnp.float32), EPN, axis=0)
    d_edge_pre, grad_edge_in, grad_edge_out = backward_mlp(
        edge_input, e_pre, e_hidden, e_linear, w_edge_out, d_edge
    )
    dx_edge = jnp.dot(d_edge_pre, w_edge_in.T, preferred_element_type=jnp.float32)
    edge_grad = (d_edge + dx_edge[:, :latent]).astype(jnp.bfloat16)
    grad_h = grad_h + dx_edge[:, 2 * latent :].reshape(node_count, EPN, latent).sum(axis=1)
    spread = jax.ops.segment_sum(dx_edge[:, latent : 2 * latent], edge_source, node_count + 2 * RIM)
    rim_terms = jnp.concatenate([spread[:RIM], spread[node_count + RIM :]], axis=0)
    rim_back = with_halo(rim_terms.astype(jnp.bfloat16), (("dom", 0),), RIM).astype(rim_terms.dtype)
    middle = jnp.zeros((node_count - 2 * RIM, latent), jnp.float32)
    grad_h = (
        grad_h
        + spread[RIM : RIM + node_count]
        + jnp.concatenate([rim_back[:RIM], middle, rim_back[3 * RIM :]], axis=0)
    )
    d_message = (
        d_contact.reshape(blocks, BLOCK * latent)[contact_block]
        .reshape(row_count * BLOCK, latent)
        .astype(jnp.float32)
    )
    d_contact_pre, grad_contact_in, grad_contact_out = backward_mlp(
        contact_input, c_pre, c_hidden, c_linear, w_contact_out, d_message
    )
    d_own = jnp.dot(d_contact_pre, w_contact_in[:latent].T, preferred_element_type=jnp.float32)
    own_sum = jnp.dot(
        block_hit.astype(jnp.float32),
        d_own.reshape(row_count, BLOCK * latent),
        precision=lax.Precision.HIGHEST,
        preferred_element_type=jnp.float32,
    )
    grad_h = grad_h + own_sum.reshape(node_count, latent)
    slot_place = slot_hit.astype(jnp.bfloat16)
    d_remote = jnp.dot(
        d_contact_pre, w_contact_in[latent:].T, preferred_element_type=jnp.float32
    ).astype(jnp.bfloat16)
    outgoing = d_remote.reshape(row_count, BLOCK * latent)
    payload = jnp.dot(slot_place, outgoing, preferred_element_type=jnp.float32).astype(jnp.bfloat16)
    returned = lax.all_to_all(
        payload.reshape(groups, CAP, BLOCK * latent), "dom", split_axis=0, concat_axis=0, tiled=True
    )
    served = returned.reshape(slot_count, BLOCK * latent)
    owner_hit = (asked_block[None, :] == lax.iota(jnp.int32, blocks)[:, None]) & asked_live[None, :]
    remote_sum = jnp.dot(owner_hit.astype(jnp.bfloat16), served, preferred_element_type=jnp.float32)
    grad_h = grad_h + remote_sum.reshape(node_count, latent)
    node_grad = grad_h.astype(jnp.bfloat16)
    summed = lax.psum(
        (
            grad_edge_in,
            grad_edge_out,
            grad_node_in,
            grad_node_out,
            grad_contact_in,
            grad_contact_out,
        ),
        "dom",
    )
    return (
        node_out,
        edge_out,
        node_grad,
        edge_grad,
        summed[0],
        summed[1],
        summed[2],
        summed[3],
        summed[4],
        summed[5],
    )


def solution(mesh):
    in_specs = (
        P(("rep", "dom"), None),
        P(("rep", "dom"), None),
        P(("rep", "dom")),
        P(("rep", "dom")),
        P(("rep", "dom"), None),
        P(("rep", "dom")),
        P("rep", None),
        P("rep", None),
        P("rep", None),
        P("rep", None),
        P("rep", None),
        P("rep", None),
        P(("rep", "dom"), None),
        P(("rep", "dom"), None),
    )
    out_specs = (
        P(("rep", "dom"), None),
        P(("rep", "dom"), None),
        P(("rep", "dom"), None),
        P(("rep", "dom"), None),
        P("rep", None),
        P("rep", None),
        P("rep", None),
        P("rep", None),
        P("rep", None),
        P("rep", None),
    )
    return jax.shard_map(
        on_device, mesh=mesh, in_specs=in_specs, out_specs=out_specs, check_vma=False
    )
```

profile of v0, /device:TPU:0, one launch (start us, length us, event | category | flops | bytes accessed | tf_op | source)
XLA Modules:
  0.0 715.4 jit_solution(10905333805391002032)
XLA Ops:
  11.5 11.5 %all-to-all-start = ((s32[64,1,2]{2,1,0:T(1,128)}), s32[64,1,2]{2,1,0:T(1,128)S(1)}, u32[]{:S(2)}, u32[]{:S(2)}) async-start(s32[64,1,2]{2,1,0:T(1,128)} %bitcast.1), calls=%async_computation | async-start | bytes 65536 | tf_op jit(solution)/shard_map/all_to_all | solution.py:103
  24.7 7.8 %all-to-all-done = s32[64,1,2]{2,1,0:T(1,128)S(1)} async-done(((s32[64,1,2]{2,1,0:T(1,128)}), s32[64,1,2]{2,1,0:T(1,128)S(1)}, u32[]{:S(2)}, u32[]{:S(2)}) %all-to-all-start) | async-done | bytes 544 | tf_op jit(solution)/shard_map/all_to_all | solution.py:103
  33.7 13.3 %gather_fusion.2 = bf16[128,49152]{1,0:T(8,128)(2,1)} fusion(bf16[2,49152]{1,0:T(2,128)(2,1)S(1)} %reshape.208, s32[1024]{0:T(1024)S(1)} %get-tuple-element.46), kind=kCustom, calls=%fused_computation.2 | custom fusion | bytes 25166336 | tf_op jit(solution)/shard_map/gather | solution.py:110
  47.0 17.0 %gather.20 = bf16[64,2,49152]{2,1,0:T(2,128)(2,1)} reshape(bf16[128,49152]{1,0:T(8,128)(2,1)} %gather_fusion.2) | data formatting | bytes 25165824 | tf_op jit(solution)/shard_map/gather | solution.py:110
  64.1 14.6 %broadcast_select_fusion = bf16[64,2,49152]{2,1,0:T(2,128)(2,1)} fusion(bf16[64,2,49152]{2,1,0:T(2,128)(2,1)} %gather.20, pred[64,2]{1,0:T(8,128)(4,1)S(1)} %copy.39), kind=kLoop, calls=%fused_computation.8 | loop fusion | flops 6291456 | bytes 25165952 | tf_op jit(solution)/shard_map/jit(_where)/select_n | solution.py:109
  78.7 5.9 all-to-all-start.1
  84.7 3.4 collective-permute-start
  97.9 52.6 %collective-permute-done = bf16[64,384]{1,0:T(8,128)(2,1)S(1)} collective-permute-done((bf16[64,384]{1,0:T(8,128)(2,1)S(1)}, bf16[64,384]{1,0:T(8,128)(2,1)S(1)}, u32[]{:S(2)}, u32[]{:S(2)}) %collective-permute-start) | collective-permute-done | bytes 49184 | tf_op jit(solution)/shard_map/ppermute | solution.py:22
  150.6 3.9 gather_fusion
  156.9 4.4 multiply_convert_fusion.5
  169.0 83.8 %all-to-all-done.1 = bf16[64,2,49152]{2,1,0:T(2,128)(2,1)} async-done(((bf16[64,2,49152]{2,1,0:T(2,128)(2,1)}), bf16[64,2,49152]{2,1,0:T(2,128)(2,1)}, u32[]{:S(2)}, u32[]{:S(2)}) %all-to-all-start.1) | async-done | bytes 12582944 | tf_op jit(solution)/shard_map/all_to_all | solution.py:112
  252.7 16.9 %reshape.210 = bf16[128,49152]{1,0:T(8,128)(2,1)} reshape(bf16[64,2,49152]{2,1,0:T(2,128)(2,1)} %all-to-all-done.1) | data formatting | bytes 25165824 | tf_op jit(solution)/shard_map/reshape | solution.py:119
  269.7 10.2 %gather_fusion.3 = bf16[16,49152]{1,0:T(8,128)(2,1)} fusion(bf16[128,49152]{1,0:T(8,128)(2,1)} %reshape.210, s32[1024]{0:T(1024)S(1)} %pad_clamp_fusion), kind=kCustom, calls=%fused_computation.3 | custom fusion | bytes 3145792 | tf_op jit(solution)/shard_map/gather | solution.py:119
  279.9 3.1 reshape.211
  285.9 5.6 multiply_convert_fusion.2
  312.9 3.1 reshape.222
  316.1 3.8 copy.41
  322.1 3.6 multiply_reduce_fusion
  337.1 9.4 %convolution_convert_fusion = bf16[128,49152]{1,0:T(8,128)(2,1)} fusion(bf16[16,49152]{1,0:T(8,128)(2,1)} %reshape.218, s32[16]{0:T(128)S(1)} %copy-done.60), kind=kOutput, calls=%fused_computation.6 | convolution fusion | flops 207620096 | bytes 14155840 | tf_op jit(solution)/shard_map/dot_general | solution.py:180
  346.5 17.0 %reshape.219 = bf16[64,2,49152]{2,1,0:T(2,128)(2,1)} reshape(bf16[128,49152]{1,0:T(8,128)(2,1)} %convolution_convert_fusion) | data formatting | bytes 25165824 | tf_op jit(solution)/shard_map/reshape | solution.py:182
  363.5 37.3 %all-to-all-start.2 = ((bf16[64,2,49152]{2,1,0:T(2,128)(2,1)}), bf16[64,2,49152]{2,1,0:T(2,128)(2,1)}, u32[]{:S(2)}, u32[]{:S(2)}) async-start(bf16[64,2,49152]{2,1,0:T(2,128)(2,1)} %reshape.219), calls=%async_computation.2 | async-start | bytes 25165824 | tf_op jit(solution)/shard_map/all_to_all | solution.py:181
  423.3 3.7 fusion.17
  427.0 3.4 reshape.216
  430.4 3.8 fusion.48
  434.3 8.2 %scatter_custom_fusion = f32[384,384]{1,0:T(8,128)} fusion(s32[1024]{0:T(1024)} %param.16, f32[1024,1152]{1,0:T(8,128)} %fusion.48, f32[]{:T(128)} %constant.25.clone.1), kind=kCustom, calls=%fused_computation.20 | custom fusion | flops 393216 | bytes 2163200 | tf_op jit(solution)/shard_map/scatter-add | solution.py:150
  443.6 4.2 collective-permute-start.2
  449.4 3.7 fusion.1
  457.4 88.7 %collective-permute-done.2 = bf16[64,384]{1,0:T(8,128)(2,1)} collective-permute-done((bf16[64,384]{1,0:T(8,128)(2,1)S(1)}, bf16[64,384]{1,0:T(8,128)(2,1)}, u32[]{:S(2)}, u32[]{:S(2)}) %collective-permute-start.2) | collective-permute-done | bytes 49184 | tf_op jit(solution)/shard_map/ppermute | solution.py:22
  547.0 28.6 %all-to-all-done.2 = bf16[64,2,49152]{2,1,0:T(2,128)(2,1)} async-done(((bf16[64,2,49152]{2,1,0:T(2,128)(2,1)}), bf16[64,2,49152]{2,1,0:T(2,128)(2,1)}, u32[]{:S(2)}, u32[]{:S(2)}) %all-to-all-start.2) | async-done | bytes 12582944 | tf_op jit(solution)/shard_map/all_to_all | solution.py:181
  575.6 16.9 %reshape.220 = bf16[128,49152]{1,0:T(8,128)(2,1)} reshape(bf16[64,2,49152]{2,1,0:T(2,128)(2,1)} %all-to-all-done.2) | data formatting | bytes 25165824 | tf_op jit(solution)/shard_map/reshape | solution.py:184
  592.6 6.5 fusion.27
  601.3 98.9 %all-reduce.3.cloned.1.call-done = (f32[1152,384]{1,0:T(8,128)}, f32[384,384]{1,0:T(8,128)}, f32[1152,384]{1,0:T(8,128)}, f32[384,384]{1,0:T(8,128)}, f32[768,384]{1,0:T(8,128)}, /*index=5*/f32[384,384]{1,0:T(8,128)}) async-done(((f32[1152,384]{1,0:T(8,128)}, f32[384,384]{1,0:T(8,128)}, f32[1152,384]{1,0:T(8,128)}, f32[384,384]{1,0:T(8,128)}, f32[768,384]{1,0:T(8,128)}, /*index=5*/f32[384,384]{1,0:T(8,128)}), ...) | async-done | bytes 6488080 | tf_op jit(solution)/shard_map/psum | solution.py:189
  (235 shorter events, 104.9 us)
Async XLA Ops:
  7.2 149.8 %copy-start = (bf16[1152,384]{1,0:T(8,128)(2,1)S(1)}, bf16[1152,384]{1,0:T(8,128)(2,1)}, u32[]{:S(2)}) copy-start(bf16[1152,384]{1,0:T(8,128)(2,1)} %param.20) | copy-start | bytes 2654212
  11.5 21.0 %all-to-all-start = ((s32[64,1,2]{2,1,0:T(1,128)}), s32[64,1,2]{2,1,0:T(1,128)S(1)}, u32[]{:S(2)}, u32[]{:S(2)}) async-start(s32[64,1,2]{2,1,0:T(1,128)} %bitcast.1), calls=%async_computation | async-start | bytes 65536 | tf_op jit(solution)/shard_map/all_to_all | solution.py:103
  32.8 14.3 %copy-start.53 = (s32[128]{0:T(128)}, s32[128]{0:T(128)S(1)}, u32[]{:S(2)}) copy-start(s32[128]{0:T(128)S(1)} %reshape.241) | copy-start | bytes 1540
  33.7 58.2 %copy-start.52 = (s32[1024]{0:T(1024)}, s32[1024]{0:T(1024)S(1)}, u32[]{:S(2)}) copy-start(s32[1024]{0:T(1024)S(1)} %get-tuple-element.47) | copy-start | bytes 12292
  78.7 5.9 copy-start.11
  78.7 174.1 %all-to-all-start.1 = ((bf16[64,2,49152]{2,1,0:T(2,128)(2,1)}), bf16[64,2,49152]{2,1,0:T(2,128)(2,1)}, u32[]{:S(2)}, u32[]{:S(2)}) async-start(bf16[64,2,49152]{2,1,0:T(2,128)(2,1)} %broadcast_select_fusion), calls=%async_computation.1 | async-start | bytes 25165824 | tf_op jit(solution)/shard_map/all_to_all | solution.py:112
  84.6 6.3 copy-start.56
  84.6 6.3 copy-start.15
  84.7 65.9 %collective-permute-start = (bf16[64,384]{1,0:T(8,128)(2,1)S(1)}, bf16[64,384]{1,0:T(8,128)(2,1)S(1)}, u32[]{:S(2)}, u32[]{:S(2)}) collective-permute-start(bf16[64,384]{1,0:T(8,128)(2,1)S(1)} %get-tuple-element.30), channel_id=1, source_target_pairs={{0,2},{2,4},{4,6},{6,8},{8,10},{10,12},{12,14},{14,16},{16,18},{18... | collective-permute-start | bytes 147464 | tf_op jit(solution)/shard_map/ppermute | solution.py:22
  88.1 62.5 %collective-permute-start.1 = (bf16[64,384]{1,0:T(8,128)(2,1)S(1)}, bf16[64,384]{1,0:T(8,128)(2,1)S(1)}, u32[]{:S(2)}, u32[]{:S(2)}) collective-permute-start(bf16[64,384]{1,0:T(8,128)(2,1)S(1)} %get-tuple-element.31), channel_id=1, source_target_pairs={{2,0},{4,2},{6,4},{8,6},{10,8},{12,10},{14,12},{16,14},{18,16},{20... | collective-permute-start | bytes 147464 | tf_op jit(solution)/shard_map/ppermute | solution.py:23
  156.9 4.4 copy-start.42
  169.0 134.2 %copy-start.28 = (bf16[256,384]{1,0:T(8,128)(2,1)}, bf16[256,384]{1,0:T(8,128)(2,1)S(1)}, u32[]{:S(2)}) copy-start(bf16[256,384]{1,0:T(8,128)(2,1)S(1)} %reduce) | copy-start | bytes 589828
  285.9 5.6 copy-start.41
  322.1 3.7 copy-start.2
  322.1 4.7 copy-start.3
  327.6 3.3 copy-start.24
  329.0 3.0 copy-start.37
  363.5 212.1 %all-to-all-start.2 = ((bf16[64,2,49152]{2,1,0:T(2,128)(2,1)}), bf16[64,2,49152]{2,1,0:T(2,128)(2,1)}, u32[]{:S(2)}, u32[]{:S(2)}) async-start(bf16[64,2,49152]{2,1,0:T(2,128)(2,1)} %reshape.219), calls=%async_computation.2 | async-start | bytes 25165824 | tf_op jit(solution)/shard_map/all_to_all | solution.py:181
  400.9 299.3 %all-reduce.3.cloned.1.call-start = ((), (), s32[]{:S(2)}) async-start(), calls=%async_computation.3 | async-start | bytes 12976128 | tf_op jit(solution)/shard_map/psum | solution.py:189
  402.4 3.0 copy-start.10
  402.4 3.0 copy-start.48
  402.4 3.0 copy-start.50
  427.0 3.4 copy-start.18
  434.3 15.1 %copy-start.5 = (f32[1024,384]{1,0:T(8,128)S(1)}, f32[1024,384]{1,0:T(8,128)}, u32[]{:S(2)}) copy-start(f32[1024,384]{1,0:T(8,128)} %reshape.213) | copy-start | bytes 4718596
  443.6 102.6 %collective-permute-start.2 = (bf16[64,384]{1,0:T(8,128)(2,1)S(1)}, bf16[64,384]{1,0:T(8,128)(2,1)}, u32[]{:S(2)}, u32[]{:S(2)}) collective-permute-start(bf16[64,384]{1,0:T(8,128)(2,1)S(1)} %get-tuple-element.26), channel_id=1, source_target_pairs={{0,2},{2,4},{4,6},{6,8},{8,10},{10,12},{12,14},{14,16},{16,18},{18... | collective-permute-start | bytes 147464 | tf_op jit(solution)/shard_map/ppermute | solution.py:22
  447.7 5.4 copy-start.58
  447.7 98.4 %collective-permute-start.3 = (bf16[64,384]{1,0:T(8,128)(2,1)S(1)}, bf16[64,384]{1,0:T(8,128)(2,1)}, u32[]{:S(2)}, u32[]{:S(2)}) collective-permute-start(bf16[64,384]{1,0:T(8,128)(2,1)S(1)} %get-tuple-element.27), channel_id=1, source_target_pairs={{2,0},{4,2},{6,4},{8,6},{10,8},{12,10},{14,12},{16,14},{18,16},{20... | collective-permute-start | bytes 147464 | tf_op jit(solution)/shard_map/ppermute | solution.py:23
  449.4 3.7 copy-start.8
  547.0 45.6 %copy-start.54 = (s32[128]{0:T(128)S(1)}, s32[128]{0:T(128)}, u32[]{:S(2)}) copy-start(s32[128]{0:T(128)} %copy-done.53) | copy-start | bytes 1540
  592.6 6.9 copy-start.13
  592.6 6.9 copy-start.21
  700.2 3.8 copy-start.19
  (42 other events, 73.0 us)
Sparse Core Ops, SparseCore 0:
  422.6 277.5 all-reduce.2
where the time goes:
time: 726 us; the launch traced here: 715 us
  waiting for transfers between devices  361 us (50%)
  local copies, waits for them, and re-layouts  163 us (22%)
  starting transfers between devices  65.6 us (9%)
  matrix products  58.9 us (8%)
  other arithmetic  52.5 us (7%)
  between operations  15.2 us (2%)
    ppermute x2, waiting for transfers between devices, with_halo(): before = lax.ppermute(last, axis, up)  141 us
    psum x1, waiting for transfers between devices, on_device(): lax.psum((grad_edge_in, grad_edge_out, grad_node_in, grad_node_out, grad_...  98.9 us
    all_to_all x1, waiting for transfers between devices, on_device(): lax.all_to_all(reply_rows.reshape(groups, CAP, BLOCK * latent), 'dom', sp...  83.8 us
    all_to_all x1, starting transfers between devices, on_device(): lax.all_to_all(payload.reshape(groups, CAP, BLOCK * latent), 'dom', split...  37.3 us
    gather x2, local copies, waits for them, and re-layouts, on_device(): block_rows[asked_block]  30.3 us
    all_to_all x1, waiting for transfers between devices, on_device(): lax.all_to_all(payload.reshape(groups, CAP, BLOCK * latent), 'dom', split...  28.6 us
    unnamed x141, local copies, waits for them, and re-layouts  21.3 us
    reshape x2, local copies, waits for them, and re-layouts, on_device(): arrived.reshape(slot_count, BLOCK * latent)[slot_index]  20 us
  transfers between devices with their start and end apart: 8, of which 6 were waited for; matrix products, arithmetic and copies ran while one was open for 14% of the time, Pallas kernels for 0%

commit v1 on v0

v1 whole, which is shorter than its diff:
```python
import functools

import jax
import jax.numpy as jnp
from jax import lax
from jax.experimental import pallas as pl
from jax.experimental.pallas import tpu as pltpu
from jax.sharding import PartitionSpec as P

L = 384
BLOCK = 128
EPN = 4
RIM = 64
NODES = 256
EDGES = 1024
ROWS = 16
TILE = 256
COLORS = 3
COLS = 128
SIDE = 4
DOM = 64
EPS = 1e-05
BF = jnp.bfloat16
F32 = jnp.float32
MESH = pl.DeviceIdType.MESH

EDGE_IN, EDGE_OUT, NODE_IN, NODE_OUT, CONTACT_IN, CONTACT_OUT = 0, 1152, 1536, 2688, 3072, 3840
GROWS = 4352
QUARTER = GROWS // 4
PIECE = QUARTER // 4

ORDERS = (("z", "x", "y"), ("x", "y", "z"), ("y", "z", "x"))
STRIDE = {"y": 16, "x": 4, "z": 1}
AXES = ("y", "x", "z")
N_CHUNK = 4
CHUNK = ROWS // N_CHUNK


def mm(a, b):
    return lax.dot_general(a, b, (((1,), (0,)), ((), ())), preferred_element_type=F32)


def mm_nt(a, b):
    return lax.dot_general(a, b, (((1,), (1,)), ((), ())), preferred_element_type=F32)


def mm_tn(a, b):
    return lax.dot_general(a, b, (((0,), (0,)), ((), ())), preferred_element_type=F32)


def row_mean(v):
    return jnp.sum(v, axis=-1, keepdims=True) * (1.0 / L)


def norm(y):
    center = y - row_mean(y)
    scale = lax.rsqrt(row_mean(center * center) + EPS)
    return center * scale, scale


def norm_back(u, scale, g):
    return scale * (g - row_mean(g) - u * row_mean(g * u))


def silu_parts(z):
    s = jax.nn.sigmoid(z)
    return (z * s).astype(BF), s * (1.0 + z * (1.0 - s))


def body(
    x_ref, src_ref, meta_ref, ncot_ref,
    es_hbm, ecot_hbm, wei_hbm, weo_hbm, wni_hbm, wno_hbm, wci_hbm, wco_hbm,
    node_out, edge_out, node_grad, edge_grad, grads_hbm,
    es, ecot, wei, weo, wni, wno, wci, wco,
    plane, sbuf, rbuf, dz_all, r2, r3, r3src,
    g1, g2src, g2, g3, gout,
    halo, rim_out, rim_in, xext, onehot,
    meta_v, meta_s, table_v, table_s,
    src_rows, tgt_rows, e_u, e_r, e_h, e_a, e_dy, e_dz, mesh_sum,
    c_u, c_r, c_h, c_a, c_dy, p_own, csum, dzown, tsum, nbuf, dcon, dmesh,
    local_sem, meta_ss, meta_rs, halo_ss, halo_rs, rim_ss, rim_rs,
    f1_ss, f1_rs, f2_ss, f2_rs, f2b_ss, f2b_rs, f3_ss, f3_rs,
    b1_ss, b1_rs, b1b_ss, b1b_rs, b2_ss, b2_rs, b3_ss, b3_rs,
    g1_ss, g1_rs, g2_ss, g2_rs, g3_ss, g3_rs, g4_ss, g4_rs, g4b_ss, g4b_rs,
    g5_ss, g5_rs, g5b_ss, g5b_rs,
):
    me = lax.axis_index("dom")
    coord = {"y": lax.div(me, 16), "x": lax.rem(lax.div(me, 4), 4), "z": lax.rem(me, 4)}

    def around(axis, off):
        return lax.rem(coord[axis] + off, SIDE)

    def peer(axis, off):
        return me + (around(axis, off) - coord[axis]) * STRIDE[axis]

    up, down = lax.rem(me + 1, DOM), lax.rem(me + DOM - 1, DOM)

    def remote(src, dst, ss, rs, dev):
        return pltpu.make_async_remote_copy(
            src_ref=src, dst_ref=dst, send_sem=ss, recv_sem=rs,
            device_id={"dom": dev}, device_id_type=MESH,
        )

    def arrived(dst, ss, rs, dev):
        remote(dst, dst, ss, rs, dev).wait_recv()

    pending = []

    def send(*args):
        copy = remote(*args)
        copy.start()
        pending.append(copy)

    def flush():
        for copy in pending:
            copy.wait_send()
        pending.clear()

    loads = [
        pltpu.make_async_copy(src, dst, local_sem.at[i])
        for i, (src, dst) in enumerate(
            [(wci_hbm, wci), (es_hbm, es), (wei_hbm, wei), (weo_hbm, weo), (wco_hbm, wco),
             (wni_hbm, wni), (wno_hbm, wno), (ecot_hbm, ecot)]
        )
    ]
    for load in loads:
        load.start()

    barrier = pltpu.get_barrier_semaphore()
    for axis in AXES:
        for off in (1, 2, 3):
            pl.semaphore_signal(barrier, inc=1, device_id={"dom": peer(axis, off)}, device_id_type=MESH)
    pl.semaphore_signal(barrier, inc=1, device_id={"dom": up}, device_id_type=MESH)
    pl.semaphore_signal(barrier, inc=1, device_id={"dom": down}, device_id_type=MESH)

    x = x_ref[...]
    for k, (a1, a2, a3) in enumerate(ORDERS):
        own = (coord[a2] * SIDE + coord[a1]) * 2
        for b in range(2):
            plane[k, own + b] = x_ref[b * BLOCK:(b + 1) * BLOCK, k * COLS:(k + 1) * COLS]
    pl.semaphore_wait(barrier, 11)

    for k, (a1, a2, a3) in enumerate(ORDERS):
        own = (coord[a2] * SIDE + coord[a1]) * 2
        for off in (1, 2, 3):
            part = plane.at[k, pl.ds(own, 2)]
            send(part, part, f1_ss.at[k, off - 1], f1_rs.at[k, off - 1], peer(a1, off))
    send(x_ref.at[pl.ds(NODES - RIM, RIM)], halo.at[0], halo_ss.at[0], halo_rs.at[0], up)
    send(x_ref.at[pl.ds(0, RIM)], halo.at[1], halo_ss.at[1], halo_rs.at[1], down)
    for i, axis in enumerate(AXES):
        meta_v[i, 0] = meta_ref[...]
        for off in (1, 2, 3):
            send(meta_ref, meta_v.at[i, SIDE - off], meta_ss.at[i, off - 1], meta_rs.at[i, off - 1], peer(axis, off))

    lanes = lax.broadcasted_iota(jnp.int32, (BLOCK, L), 1)
    idx = jnp.concatenate([src_ref[...].astype(F32)] * 16, axis=0).T
    for j in range(EDGES // BLOCK):
        col = idx[:, j:j + 1].astype(jnp.int32)
        onehot[j * BLOCK:(j + 1) * BLOCK, :] = jnp.where(col == lanes, 1.0, 0.0).astype(BF)
    for k in range(COLORS):
        for j in range(SIDE):
            dz_all[k, j, ROWS] = jnp.zeros((BLOCK, COLS), BF)
    csum[...] = jnp.zeros_like(csum)
    dzown[...] = jnp.zeros_like(dzown)
    loads[0].wait()
    p_own[...] = mm(x, wci[0:L]).reshape(2, BLOCK, L)

    for k, (a1, a2, a3) in enumerate(ORDERS):
        for off in (1, 2, 3):
            got = (coord[a2] * SIDE + around(a1, SIDE - off)) * 2
            arrived(plane.at[k, pl.ds(got, 2)], f1_ss.at[k, off - 1], f1_rs.at[k, off - 1], peer(a1, off))
        part = plane.at[k, pl.ds(coord[a2] * 8, 8)]
        send(part, part, f2_ss.at[k, 0], f2_rs.at[k, 0], peer(a2, 1))
        send(part, part, f2_ss.at[k, 1], f2_rs.at[k, 1], peer(a2, 3))

    arrived(halo.at[0], halo_ss.at[0], halo_rs.at[0], up)
    arrived(halo.at[1], halo_ss.at[1], halo_rs.at[1], down)
    has_low = (me > 0).astype(F32)
    has_high = (me < DOM - 1).astype(F32)
    xext[0:RIM] = (halo[0].astype(F32) * has_low).astype(BF)
    xext[RIM:RIM + NODES] = x
    xext[RIM + NODES:] = (halo[1].astype(F32) * has_high).astype(BF)

    for load in loads[1:4]:
        load.wait()

    quarter = TILE // EPN
    fan = jnp.where(
        lax.div(lax.broadcasted_iota(jnp.int32, (TILE, quarter), 0), EPN)
        == lax.broadcasted_iota(jnp.int32, (TILE, quarter), 1), 1.0, 0.0,
    ).astype(BF)

    def edge_forward(t):
        rows = pl.ds(pl.multiple_of(t * TILE, TILE), TILE)
        nodes = pl.ds(pl.multiple_of(t * quarter, quarter), quarter)
        state = es[rows]
        src = mm(onehot[rows], xext[...]).astype(BF)
        tgt = mm(fan, x_ref[nodes]).astype(BF)
        z = mm(state, wei[0:L]) + mm(src, wei[L:2 * L]) + mm(tgt, wei[2 * L:])
        a, h = silu_parts(z)
        u, r = norm(mm(a, weo[...]))
        out = (state.astype(F32) + u).astype(BF)
        edge_out[rows] = out
        mesh_sum[nodes] = mm_tn(fan, out).astype(BF)
        e_a[rows] = a
        e_h[rows] = h
        e_u[rows] = u
        e_r[rows] = r

    pl.loop(0, 2)(edge_forward)

    for k, (a1, a2, a3) in enumerate(ORDERS):
        low = pl.ds(around(a2, 3) * 8, 8)
        high = pl.ds(around(a2, 1) * 8, 8)
        arrived(plane.at[k, low], f2_ss.at[k, 0], f2_rs.at[k, 0], peer(a2, 1))
        part = plane.at[k, pl.ds(around(a2, 3) * 8, 4)]
        send(part, part, f2b_ss.at[k, 0], f2b_rs.at[k, 0], peer(a2, 1))
        arrived(plane.at[k, high], f2_ss.at[k, 1], f2_rs.at[k, 1], peer(a2, 3))
        part = plane.at[k, pl.ds(around(a2, 1) * 8 + 4, 4)]
        send(part, part, f2b_ss.at[k, 1], f2b_rs.at[k, 1], peer(a2, 3))

    for i, axis in enumerate(AXES):
        for off in (1, 2, 3):
            arrived(meta_v.at[i, SIDE - off], meta_ss.at[i, off - 1], meta_rs.at[i, off - 1], peer(axis, off))
    lane = lax.broadcasted_iota(jnp.int32, (1, 128), 1)
    mine = [coord[a3] * 32 for a1, a2, a3 in ORDERS]
    sought = lax.rem(lane, 32) + jnp.where(lane < 32, mine[0], jnp.where(lane < 64, mine[1], mine[2]))
    place = lax.broadcasted_iota(jnp.int32, (ROWS, 128), 1)
    for j in range(SIDE):
        asked = [meta_v[AXES.index(a3), j, 8:8 + ROWS] for a1, a2, a3 in ORDERS]
        asked = jnp.where(place < 32, asked[0], jnp.where(place < 64, asked[1], asked[2]))
        first = second = jnp.full((1, 128), ROWS, jnp.int32)
        for c in reversed(range(ROWS)):
            hit = asked[c:c + 1] == sought
            second = jnp.where(hit, first, second)
            first = jnp.where(hit, c, first)
        table_v[2 * j:2 * j + 1] = first
        table_v[2 * j + 1:2 * j + 2] = second
    to_smem = [
        pltpu.make_async_copy(meta_v, meta_s, local_sem.at[8]),
        pltpu.make_async_copy(table_v, table_s, local_sem.at[9]),
    ]
    for copy in to_smem:
        copy.start()

    pl.loop(2, 4)(edge_forward)

    for copy in to_smem:
        copy.wait()
    for k, (a1, a2, a3) in enumerate(ORDERS):
        opposite = around(a2, 2) * 8
        arrived(plane.at[k, pl.ds(opposite, 4)], f2b_ss.at[k, 0], f2b_rs.at[k, 0], peer(a2, 1))
        arrived(plane.at[k, pl.ds(opposite + 4, 4)], f2b_ss.at[k, 1], f2b_rs.at[k, 1], peer(a2, 3))

    for q in range(N_CHUNK):
        for j in (2, 1, 3, 0):
            for k, (a1, a2, a3) in enumerate(ORDERS):
                i = AXES.index(a3)
                for c in range(CHUNK):
                    slot = meta_s[i, j, k, q * CHUNK + c]
                    if j:
                        sbuf[k, j - 1, q * CHUNK + c] = plane[k, slot]
                    else:
                        rbuf[q][k, 0, c] = plane[k, slot]
                if j:
                    send(
                        sbuf.at[k, j - 1, pl.ds(q * CHUNK, CHUNK)], rbuf[q].at[k, SIDE - j],
                        f3_ss.at[q, k, j - 1], f3_rs.at[q, k, j - 1], peer(a3, j),
                    )

    loads[4].wait()
    for q in range(N_CHUNK):
        for k, (a1, a2, a3) in enumerate(ORDERS):
            for j in (1, 2, 3):
                arrived(rbuf[q].at[k, SIDE - j], f3_ss.at[q, k, j - 1], f3_rs.at[q, k, j - 1], peer(a3, j))

        @pl.loop(0, CHUNK // 2)
        def _(p):
            parts, owns, weights = [], [], []
            for s in range(2):
                c = q * CHUNK + 2 * p + s
                cols = []
                for k, (a1, a2, a3) in enumerate(ORDERS):
                    where = lax.rem(meta_s[0, 0, 3 + k, c] - coord[a3] + SIDE, SIDE)
                    cols.append(rbuf[q][k, where, 2 * p + s])
                parts.append(jnp.concatenate(cols, axis=1))
                block = meta_s[0, 0, 6, c]
                owns.append(p_own[block])
                weights.append(block.astype(F32))
            rows = pl.ds(pl.multiple_of(q * CHUNK * BLOCK + p * TILE, TILE), TILE)
            z = mm(jnp.concatenate(parts, axis=0), wci[L:]) + jnp.concatenate(owns, axis=0)
            a, h = silu_parts(z)
            u, r = norm(mm(a, wco[...]))
            c_a[rows] = a
            c_h[rows] = h
            c_u[rows] = u
            c_r[rows] = r
            message = u.astype(BF).astype(F32)
            for s in range(2):
                m = message[s * BLOCK:(s + 1) * BLOCK]
                csum[1] += m * weights[s]
                csum[0] += m * (1.0 - weights[s])

    loads[5].wait()
    loads[6].wait()
    nbuf[:, 0:L] = x
    nbuf[:, L:2 * L] = mesh_sum[...]
    nbuf[:, 2 * L:] = csum[...].reshape(NODES, L).astype(BF)
    a, h = silu_parts(mm(nbuf[...], wni[...]))
    u, r = norm(mm(a, wno[...]))
    node_out[...] = (x.astype(F32) + u).astype(BF)
    ncot = ncot_ref[...].astype(F32)
    n_dy = norm_back(u, r, ncot).astype(BF)
    n_dz = (mm_nt(n_dy, wno[...]) * h).astype(BF)
    dcon[...] = mm_nt(n_dz, wni[2 * L:]).astype(BF).reshape(2, BLOCK, L)

    @pl.loop(0, ROWS // 2)
    def _(t):
        rows = pl.ds(pl.multiple_of(t * TILE, TILE), TILE)
        blocks = [meta_s[0, 0, 6, 2 * t + s] for s in range(2)]
        g = jnp.concatenate([dcon[b] for b in blocks], axis=0).astype(F32)
        dy = norm_back(c_u[rows], c_r[rows], g).astype(BF)
        c_dy[rows] = dy
        dz = (mm_nt(dy, wco[...]) * c_h[rows]).astype(BF)
        for s in range(2):
            part = dz[s * BLOCK:(s + 1) * BLOCK]
            weight = blocks[s].astype(F32)
            dzown[1] += part.astype(F32) * weight
            dzown[0] += part.astype(F32) * (1.0 - weight)
            for k in range(COLORS):
                dz_all[k, 0, 2 * t + s] = part[:, k * COLS:(k + 1) * COLS]
        for k, (a1, a2, a3) in enumerate(ORDERS):
            pair = pl.ds(2 * t, 2)
            remote(dz_all.at[k, 0, pair], dz_all.at[k, 3, pair], b1_ss.at[k, 0, t], b1_rs.at[k, 0, t], peer(a3, 1)).start()
            remote(dz_all.at[k, 0, pair], dz_all.at[k, 1, pair], b1_ss.at[k, 1, t], b1_rs.at[k, 1, t], peer(a3, 3)).start()

    def put(row, value):
        value = value.astype(BF)
        count = value.shape[0]
        for k in range(COLORS):
            sbuf_rows = value[:, k * COLS:(k + 1) * COLS].reshape(count // BLOCK, BLOCK, COLS)
            for i in range(count // BLOCK):
                g = row // BLOCK + i
                gsend(k, g)[...] = sbuf_rows[i]

    flush()

    def gsend(k, g):
        return sbuf.at[k, g // ROWS, g % ROWS]

    dmesh[...] = mm_nt(n_dz, wni[L:2 * L]).astype(BF)
    loads[7].wait()

    def edge_backward(t):
        rows = pl.ds(pl.multiple_of(t * TILE, TILE), TILE)
        nodes = pl.ds(pl.multiple_of(t * quarter, quarter), quarter)
        g = ecot[rows].astype(F32) + mm(fan, dmesh[nodes])
        dy = norm_back(e_u[rows], e_r[rows], g).astype(BF)
        dz = (mm_nt(dy, weo[...]) * e_h[rows]).astype(BF)
        edge_grad[rows] = (g + mm_nt(dz, wei[0:L])).astype(BF)
        tsum[nodes] = mm_tn(fan, dz).astype(BF)
        e_dy[rows] = dy
        e_dz[rows] = dz

    @pl.loop(0, 4)
    def _(t):
        edge_backward(t)
        for k, (a1, a2, a3) in enumerate(ORDERS):
            pair = pl.ds(2 * t, 2)
            arrived(dz_all.at[k, 3, pair], b1_ss.at[k, 0, t], b1_rs.at[k, 0, t], peer(a3, 1))
            remote(dz_all.at[k, 3, pair], dz_all.at[k, 2, pair], b1b_ss.at[k, t], b1b_rs.at[k, t], peer(a3, 1)).start()
            late = t + 4
            pair = pl.ds(2 * late, 2)
            arrived(dz_all.at[k, 1, pair], b1_ss.at[k, 1, late], b1_rs.at[k, 1, late], peer(a3, 3))
            remote(dz_all.at[k, 1, pair], dz_all.at[k, 2, pair], b1b_ss.at[k, late], b1b_rs.at[k, late], peer(a3, 3)).start()

    spread = mm_tn(onehot[...], e_dz[...])
    spread_low = spread.astype(BF)
    rim_out[0] = spread_low[0:RIM]
    rim_out[1] = spread_low[RIM + NODES:]
    send(rim_out.at[0], rim_in.at[0], rim_ss.at[0], rim_rs.at[0], down)
    send(rim_out.at[1], rim_in.at[1], rim_ss.at[1], rim_rs.at[1], up)
    put(EDGE_IN + L, mm_tn(xext[...], spread_low))
    put(EDGE_IN, mm_tn(es[...], e_dz[...]))
    put(EDGE_IN + 2 * L, mm_tn(x, tsum[...]))
    put(EDGE_OUT, mm_tn(e_a[...], e_dy[...]))

    @pl.loop(0, 4)
    def _(t):
        late = t + 4
        for k, (a1, a2, a3) in enumerate(ORDERS):
            arrived(dz_all.at[k, 3, pl.ds(2 * late, 2)], b1_ss.at[k, 0, late], b1_rs.at[k, 0, late], peer(a3, 1))
            arrived(dz_all.at[k, 1, pl.ds(2 * t, 2)], b1_ss.at[k, 1, t], b1_rs.at[k, 1, t], peer(a3, 3))
            arrived(dz_all.at[k, 2, pl.ds(2 * t, 2)], b1b_ss.at[k, t], b1b_rs.at[k, t], peer(a3, 1))
            arrived(dz_all.at[k, 2, pl.ds(2 * late, 2)], b1b_ss.at[k, late], b1b_rs.at[k, late], peer(a3, 3))

    @pl.loop(0, 2 * 16)
    def _(s):
        for k in range(COLORS):
            total = jnp.zeros((BLOCK, COLS), F32)
            for j in range(SIDE):
                for i in range(2):
                    total += dz_all[k, j, table_s[2 * j + i, k * 32 + s]].astype(F32)
            plane[k, s] = total.astype(BF)

    for k, (a1, a2, a3) in enumerate(ORDERS):
        for off in (2, 1, 3):
            send(
                plane.at[k, pl.ds(around(a2, off) * 8, 8)], r2.at[k, off - 1],
                b2_ss.at[k, off - 1], b2_rs.at[k, off - 1], peer(a2, off),
            )
    put(CONTACT_OUT, mm_tn(c_a[...], c_dy[...]))
    put(CONTACT_IN, mm_tn(x, dzown[...].reshape(NODES, L).astype(BF)))
    put(NODE_OUT, mm_tn(a, n_dy))
    for i in range(3):
        put(NODE_IN + i * L, mm_tn(nbuf[:, i * L:(i + 1) * L], n_dz))
    grad = ncot + mm_nt(n_dz, wni[0:L]) + mm_nt(tsum[...], wei[2 * L:])
    grad += mm_nt(dzown[...].reshape(NODES, L).astype(BF), wci[0:L])

    for k, (a1, a2, a3) in enumerate(ORDERS):
        for off in (1, 2, 3):
            arrived(r2.at[k, off - 1], b2_ss.at[k, off - 1], b2_rs.at[k, off - 1], peer(a2, off))

        @pl.loop(0, 8)
        def _(s):
            total = plane[k, coord[a2] * 8 + s].astype(F32)
            for o in range(3):
                total += r2[k, o, s].astype(F32)
            r3src[k, s] = total.astype(BF)

        for off in (1, 2, 3):
            send(
                r3src.at[k, pl.ds(around(a1, off) * 2, 2)], r3.at[k, off - 1],
                b3_ss.at[k, off - 1], b3_rs.at[k, off - 1], peer(a1, off),
            )
    arrived(rim_in.at[0], rim_ss.at[0], rim_rs.at[0], down)
    arrived(rim_in.at[1], rim_ss.at[1], rim_rs.at[1], up)
    first = spread[RIM:2 * RIM] + rim_in[1].astype(F32) * has_low
    last = spread[NODES:NODES + RIM] + rim_in[0].astype(F32) * has_high
    own_spread = jnp.concatenate([first, spread[2 * RIM:NODES], last], axis=0).astype(BF)
    grad += mm_nt(own_spread, wei[L:2 * L])
    cols = []
    for k, (a1, a2, a3) in enumerate(ORDERS):
        halves = [r3src[k, coord[a1] * 2 + b].astype(F32) for b in range(2)]
        for off in (1, 2, 3):
            arrived(r3.at[k, off - 1], b3_ss.at[k, off - 1], b3_rs.at[k, off - 1], peer(a1, off))
            halves = [halves[b] + r3[k, off - 1, b].astype(F32) for b in range(2)]
        cols.append(jnp.concatenate(halves, axis=0).astype(BF))
    s_rem = jnp.concatenate(cols, axis=1)
    put(CONTACT_IN + L, mm_tn(x, s_rem))
    node_grad[...] = (grad + mm_nt(s_rem, wci[L:])).astype(BF)

    def rows_of(k, quarter_index):
        return gflat.at[k, pl.ds(quarter_index * QUARTER, QUARTER)]

    gflat = sbuf.reshape(COLORS, 3 * ROWS * BLOCK, COLS)
    for k, (a1, a2, a3) in enumerate(ORDERS):
        for off in (2, 1, 3):
            send(rows_of(k, around(a3, off)), g1.at[k, off - 1], g1_ss.at[k, off - 1], g1_rs.at[k, off - 1], peer(a3, off))
    for k, (a1, a2, a3) in enumerate(ORDERS):
        for off in (1, 2, 3):
            arrived(g1.at[k, off - 1], g1_ss.at[k, off - 1], g1_rs.at[k, off - 1], peer(a3, off))

        @pl.loop(0, 4)
        def _(t):
            rows = pl.ds(pl.multiple_of(t * PIECE, 16), PIECE)
            total = gflat[k, pl.ds(pl.multiple_of(coord[a3] * QUARTER + t * PIECE, 16), PIECE)].astype(F32)
            for o in range(3):
                total += g1[k, o, rows].astype(F32)
            g2src[k, t] = total.astype(BF)

        for off in (2, 1, 3):
            send(g2src.at[k, around(a2, off)], g2.at[k, off - 1], g2_ss.at[k, off - 1], g2_rs.at[k, off - 1], peer(a2, off))
    for k, (a1, a2, a3) in enumerate(ORDERS):
        for off in (1, 2, 3):
            arrived(g2.at[k, off - 1], g2_ss.at[k, off - 1], g2_rs.at[k, off - 1], peer(a2, off))
        total = g2src[k, coord[a2]].astype(F32)
        for o in range(3):
            total += g2[k, o].astype(F32)
        g3[k, coord[a1]] = total.astype(BF)
        for off in (2, 1, 3):
            part = g3.at[k, coord[a1]]
            send(part, part, g3_ss.at[k, off - 1], g3_rs.at[k, off - 1], peer(a1, off))
    for k, (a1, a2, a3) in enumerate(ORDERS):
        for off in (1, 2, 3):
            arrived(g3.at[k, around(a1, SIDE - off)], g3_ss.at[k, off - 1], g3_rs.at[k, off - 1], peer(a1, off))
        total = g3[k, 0].astype(F32)
        for o in range(1, SIDE):
            total += g3[k, o].astype(F32)
        gout[k, coord[a3], coord[a2]] = total.astype(BF)
        part = gout.at[k, coord[a3], coord[a2]]
        for off in (2, 1, 3):
            send(part, part, g4_ss.at[k, off - 1], g4_rs.at[k, off - 1], peer(a2, off))
    for k, (a1, a2, a3) in enumerate(ORDERS):
        for off in (1, 2, 3):
            arrived(
                gout.at[k, coord[a3], around(a2, SIDE - off)],
                g4_ss.at[k, off - 1], g4_rs.at[k, off - 1], peer(a2, off),
            )
        part = gout.at[k, coord[a3]]
        send(part, part, g5_ss.at[k, 0], g5_rs.at[k, 0], peer(a3, 1))
        send(part, part, g5_ss.at[k, 1], g5_rs.at[k, 1], peer(a3, 3))
    for k, (a1, a2, a3) in enumerate(ORDERS):
        arrived(gout.at[k, around(a3, 3)], g5_ss.at[k, 0], g5_rs.at[k, 0], peer(a3, 1))
        part = gout.at[k, around(a3, 3), pl.ds(0, 2)]
        send(part, part, g5b_ss.at[k, 0], g5b_rs.at[k, 0], peer(a3, 1))
        arrived(gout.at[k, around(a3, 1)], g5_ss.at[k, 1], g5_rs.at[k, 1], peer(a3, 3))
        part = gout.at[k, around(a3, 1), pl.ds(2, 2)]
        send(part, part, g5b_ss.at[k, 1], g5b_rs.at[k, 1], peer(a3, 3))
    for k, (a1, a2, a3) in enumerate(ORDERS):
        arrived(gout.at[k, around(a3, 2), pl.ds(0, 2)], g5b_ss.at[k, 0], g5b_rs.at[k, 0], peer(a3, 1))
        arrived(gout.at[k, around(a3, 2), pl.ds(2, 2)], g5b_ss.at[k, 1], g5b_rs.at[k, 1], peer(a3, 3))
    out = pltpu.make_async_copy(gout, grads_hbm, local_sem.at[10])
    out.start()

    @pl.loop(0, 8)
    def _(t):
        for k, (a1, a2, a3) in enumerate(ORDERS):
            part = dz_all.at[k, 0, pl.ds(2 * t, 2)]
            remote(part, part, b1_ss.at[k, 0, t], b1_rs.at[k, 0, t], peer(a3, 1)).wait_send()
            remote(part, part, b1_ss.at[k, 1, t], b1_rs.at[k, 1, t], peer(a3, 3)).wait_send()
            remote(part, part, b1b_ss.at[k, t], b1b_rs.at[k, t], peer(a3, 1)).wait_send()

    flush()
    out.wait()


def dma(*shape):
    return pltpu.SemaphoreType.DMA(shape)


def vm(shape, dtype):
    return pltpu.VMEM(shape, dtype)


def fused(x, src, meta, ncot, es, ecot, wei, weo, wni, wno, wci, wco):
    tile = (BLOCK, COLS)
    scratch = [
        vm((EDGES, L), BF), vm((EDGES, L), BF), vm((3 * L, L), BF), vm((L, L), BF), vm((3 * L, L), BF),
        vm((L, L), BF), vm((2 * L, L), BF), vm((L, L), BF),
        vm((COLORS, 32) + tile, BF),
        vm((COLORS, 3, ROWS) + tile, BF),
        [vm((COLORS, SIDE, CHUNK) + tile, BF) for _ in range(N_CHUNK)],
        vm((COLORS, SIDE, ROWS + 1) + tile, BF),
        vm((COLORS, 3, 8) + tile, BF), vm((COLORS, 3, 2) + tile, BF), vm((COLORS, 8) + tile, BF),
        vm((COLORS, 3, QUARTER, COLS), BF), vm((COLORS, SIDE, PIECE, COLS), BF), vm((COLORS, 3, PIECE, COLS), BF),
        vm((COLORS, SIDE, PIECE, COLS), BF), vm((COLORS, SIDE, SIDE, PIECE, COLS), BF),
        vm((2, RIM, L), BF), vm((2, RIM, L), BF), vm((2, RIM, L), BF), vm((NODES + 2 * RIM, L), BF), vm((EDGES, L), BF),
        vm((3, SIDE, 24, 128), jnp.int32), pltpu.SMEM((3, SIDE, 24, 128), jnp.int32),
        vm((8, 128), jnp.int32), pltpu.SMEM((8, 128), jnp.int32),
        vm((16, 128), BF), vm((16, 128), BF), vm((EDGES, L), F32), vm((EDGES, 1), F32), vm((EDGES, L), F32), vm((EDGES, L), BF),
        vm((EDGES, L), BF), vm((EDGES, L), BF), vm((NODES, L), BF),
        vm((ROWS * BLOCK, L), F32), vm((ROWS * BLOCK, 1), F32), vm((ROWS * BLOCK, L), F32), vm((ROWS * BLOCK, L), BF),
        vm((ROWS * BLOCK, L), BF), vm((2, BLOCK, L), F32), vm((2, BLOCK, L), F32), vm((2, BLOCK, L), F32),
        vm((NODES, L), BF), vm((NODES, 3 * L), BF), vm((2, BLOCK, L), BF), vm((NODES, L), BF),
        dma(11), dma(3, 3), dma(3, 3), dma(2), dma(2), dma(2), dma(2),
        dma(3, 3), dma(3, 3), dma(3, 2), dma(3, 2), dma(3, 2), dma(3, 2), dma(N_CHUNK, 3, 3), dma(N_CHUNK, 3, 3),
        dma(3, 2, 8), dma(3, 2, 8), dma(3, 8), dma(3, 8), dma(3, 3), dma(3, 3), dma(3, 3), dma(3, 3),
        dma(3, 3), dma(3, 3), dma(3, 3), dma(3, 3), dma(3, 3), dma(3, 3), dma(3, 3), dma(3, 3), dma(3, 2), dma(3, 2),
        dma(3, 2), dma(3, 2), dma(3, 2), dma(3, 2),
    ]
    here = pl.BlockSpec(memory_space=pltpu.VMEM)
    there = pl.BlockSpec(memory_space=pl.ANY)
    return pl.pallas_call(
        body,
        out_shape=(
            jax.ShapeDtypeStruct((NODES, L), BF), jax.ShapeDtypeStruct((EDGES, L), BF),
            jax.ShapeDtypeStruct((NODES, L), BF), jax.ShapeDtypeStruct((EDGES, L), BF),
            jax.ShapeDtypeStruct((COLORS, SIDE, SIDE, PIECE, COLS), BF),
        ),
        in_specs=[here] * 4 + [there] * 8,
        out_specs=[here] * 4 + [there],
        scratch_shapes=scratch,
        compiler_params=pltpu.CompilerParams(
            collective_id=0, has_side_effects=True, vmem_limit_bytes=63 * 1024 * 1024
        ),
        name="layer",
    )(x, src, meta, ncot, es, ecot, wei, weo, wni, wno, wci, wco)


def on_device(
    node_state, edge_state, edge_source, contact_block, contact_host, contact_remote,
    w_edge_in, w_edge_out, w_node_in, w_node_out, w_contact_in, w_contact_out, node_cot, edge_cot,
):
    host = contact_host[:, 0]
    hy, hx, hz = host // 16, host // 4 % 4, host % 4
    at = {"y": hy, "x": hx, "z": hz}
    lines = [(at[a2] * SIDE + at[a1]) * 2 + contact_remote for a1, a2, a3 in ORDERS]
    lines += [at[a3] for a1, a2, a3 in ORDERS]
    lines += [contact_block, contact_block]
    meta = jnp.pad(jnp.stack(lines), ((0, 0), (0, 128 - ROWS)))
    asked = [jnp.broadcast_to((lines[3 + k] * 32 + lines[k])[:, None], (ROWS, 32)) for k in (0, 1, 2, 2)]
    meta = jnp.concatenate([meta, jnp.concatenate(asked, axis=1)], axis=0)
    node_out, edge_out, node_grad, edge_grad, packed = fused(
        node_state, edge_source.reshape(8, 128), meta, node_cot, edge_state, edge_cot,
        w_edge_in, w_edge_out, w_node_in, w_node_out, w_contact_in, w_contact_out,
    )
    packed = packed.reshape(COLORS, GROWS, COLS)

    def grad(row, count):
        return jnp.concatenate([packed[k, row:row + count] for k in range(COLORS)], axis=1).astype(F32)

    return (
        node_out, edge_out, node_grad, edge_grad,
        grad(EDGE_IN, 3 * L), grad(EDGE_OUT, L), grad(NODE_IN, 3 * L), grad(NODE_OUT, L),
        grad(CONTACT_IN, 2 * L), grad(CONTACT_OUT, L),
    )


def solution(mesh):
    rows = P(("rep", "dom"), None)
    flat = P(("rep", "dom"))
    weight = P("rep", None)
    return jax.shard_map(
        on_device,
        mesh=mesh,
        in_specs=(rows, rows, flat, flat, rows, flat) + (weight,) * 6 + (rows, rows),
        out_specs=(rows,) * 4 + (weight,) * 6,
        check_vma=False,
    )
```

time: 726 us -> 155 us (0.21); the launches traced: 715 us -> 155 us
  waiting for transfers between devices: 361 us -> 0 us
  local copies, waits for them, and re-layouts: 163 us -> 6.99 us
  Pallas kernels: 0 us -> 140 us
  starting transfers between devices: 65.6 us -> 0 us
  matrix products: 58.9 us -> 0 us
  other arithmetic: 52.5 us -> 7.77 us
  between operations: 15.2 us -> 0.69 us
    ppermute x4 -> x0, waiting for transfers between devices: 141 us -> none  [the longest x2 141 us: with_halo(): before = lax.ppermute(last, axis, up)]
    pallas_call x0 -> x1, Pallas kernels: none -> 140 us  [fused(): pl.pallas_call(body, out_shape=(jax.ShapeDtypeStruct((NODES, L), BF), jax...]
    all_to_all x3 -> x0, waiting for transfers between devices: 120 us -> none  [the longest x1 83.8 us: on_device(): lax.all_to_all(reply_rows.reshape(groups, CAP, BLOCK * latent), 'dom', sp...]
    psum x1 -> x0, waiting for transfers between devices: 98.9 us -> none  [on_device(): lax.psum((grad_edge_in, grad_edge_out, grad_node_in, grad_node_out, grad_...]
    reshape x16 -> x0, local copies, waits for them, and re-layouts: 74.7 us -> none  [the longest x2 20 us: on_device(): arrived.reshape(slot_count, BLOCK * latent)[slot_index]]
    dot_general x23 -> x0, matrix products: 58.9 us -> none  [the longest x3 11.7 us: forward_mlp(): hidden_pre = jnp.dot(inputs, w_first, preferred_element_type=jnp.float32)]
    all_to_all x3 -> x0, starting transfers between devices: 54.8 us -> none  [the longest x1 37.3 us: on_device(): lax.all_to_all(payload.reshape(groups, CAP, BLOCK * latent), 'dom', split...]
    gather x6 -> x0, local copies, waits for them, and re-layouts: 50 us -> none  [the longest x2 30.3 us: on_device(): block_rows[asked_block]]
  transfers between devices with their start and end apart: 8 -> 0, of which waited for: 6 -> 0; matrix products, arithmetic and copies ran while one was open for 14% -> 0% of each run, Pallas kernels for 0% -> 0%
where the time goes in v1:
time: 155 us
  Pallas kernels  140 us (90%)
  other arithmetic  7.77 us (5%)
  local copies, waits for them, and re-layouts  6.99 us (5%)
    pallas_call x1, Pallas kernels, fused(): pl.pallas_call(body, out_shape=(jax.ShapeDtypeStruct((NODES, L), BF), jax...  140 us
    convert_element_type x4, other arithmetic, grad(): jnp.concatenate([packed[k, row:row + count] for k in range(COLORS)], axis=1)  5.05 us
    unnamed x14, local copies, waits for them, and re-layouts  3.13 us

profile of v1, /device:TPU:0, one launch (start us, length us, event | category | flops | bytes accessed | tf_op | source)
XLA Modules:
  0.0 155.0 jit_solution(3553637253387787065)
XLA Ops:
  0.6 0.7 and_select_fusion
  1.3 0.7 multiply_add_fusion.2
  2.0 0.7 multiply_add_fusion
  2.7 0.8 stack.23
  3.4 0.1 broadcast_in_dim.8
  3.5 0.1 broadcast_in_dim.6
  3.6 0.1 broadcast_in_dim.7
  3.6 0.7 pad_add_fusion.meta_ref
  4.3 139.6 %layer.1 = (bf16[256,384]{1,0:T(8,128)(2,1)}, bf16[1024,384]{1,0:T(8,128)(2,1)}, bf16[256,384]{1,0:T(8,128)(2,1)}, bf16[1024,384]{1,0:T(8,128)(2,1)}, bf16[3,4,4,272,128]{4,3,2,1,0:T(8,128)(2,1)}) custom-call(bf16[256,384]{1,0:T(8,128)(2,1)} %x_ref.1, s32[8,128]{1,0:T(8,128)} %bitcast.100, s32[24,128]{1,0:T(8,128)} %pad_add_fusion.meta_ref, ...), custom_call_target="tpu_custom_call" | custom-call | tf_op jit(solution)/shard_map/layer/pallas_call | solution.py:564
  143.9 1.2 slice_bitcast_fusion.8
  145.1 0.0 copy-start
  145.1 1.1 maximum_convert_fusion.2
  146.2 1.6 %slice_bitcast_fusion.11 = (bf16[384,128]{1,0:T(8,128)(2,1)S(1)}, bf16[384,128]{1,0:T(8,128)(2,1)S(1)}, bf16[384,128]{1,0:T(8,128)(2,1)S(1)}, bf16[384,128]{1,0:...) fusion(bf16[3,4352,128]{2,1,0:T(8,128)(2,1)} %bitcast.98), kind=kLoop, calls=%fused_computation.17 | loop fusion | bytes 1769472 | tf_op jit(solution)/shard_map/squeeze | solution.py:601
  147.8 0.0 copy-done
  147.8 0.1 slice_bitcast_fusion.2
  147.9 0.9 maximum_convert_fusion.5
  148.8 1.1 maximum_convert_fusion.3
  149.9 0.0 copy-start.4
  149.9 0.0 copy-start.2
  149.9 2.0 %maximum_convert_fusion = (f32[1152,384]{1,0:T(8,128)}, f32[1152,384]{1,0:T(8,128)}) fusion(bf16[1152,128]{1,0:T(8,128)(2,1)S(1)} %get-tuple-element.44, bf16[1152,128]{1,0:T(8,128)(2,1)S(1)} %get-tuple-element.45, bf16[1152,128]{1,0:T(8,128)(2,1)S(1)} %get-tuple-element.46, bf16[1152,128]{1,0:T(8,128)(2,1)S(1)} %get-tuple-element.42, ...), kind=kLoop, calls=%fused_computation | loop fusion | flops 5308416 | bytes 5308416 | tf_op jit(solution)/shard_map/convert_element_type | solution.py:601
  151.9 0.0 copy-start.3
  151.9 0.0 copy-start.1
  151.9 0.0 copy-done.4
  151.9 0.7 copy.28
  152.6 0.0 copy-done.2
  152.6 0.9 copy.29
  153.5 0.0 copy-done.3
  153.5 0.7 copy.30
  154.2 0.0 copy-done.1
  154.2 0.9 copy.31
Async XLA Ops:
  145.1 2.7 %copy-start = (bf16[3,4,4,272,128]{4,3,2,1,0:T(8,128)(2,1)S(1)}, bf16[3,4,4,272,128]{4,3,2,1,0:T(8,128)(2,1)}, u32[]{:S(2)}) copy-start(bf16[3,4,4,272,128]{4,3,2,1,0:T(8,128)(2,1)} %get-tuple-element.19) | copy-start | bytes 10027012
  149.9 2.0 %copy-start.4 = (bf16[256,384]{1,0:T(8,128)(2,1)S(1)}, bf16[256,384]{1,0:T(8,128)(2,1)}, u32[]{:S(2)}) copy-start(bf16[256,384]{1,0:T(8,128)(2,1)} %get-tuple-element.66) | copy-start | bytes 589828
  149.9 2.7 %copy-start.2 = (bf16[1024,384]{1,0:T(8,128)(2,1)S(1)}, bf16[1024,384]{1,0:T(8,128)(2,1)}, u32[]{:S(2)}) copy-start(bf16[1024,384]{1,0:T(8,128)(2,1)} %get-tuple-element.67) | copy-start | bytes 2359300
  151.9 1.6 %copy-start.3 = (bf16[256,384]{1,0:T(8,128)(2,1)S(1)}, bf16[256,384]{1,0:T(8,128)(2,1)}, u32[]{:S(2)}) copy-start(bf16[256,384]{1,0:T(8,128)(2,1)} %get-tuple-element.68) | copy-start | bytes 589828
  151.9 2.2 %copy-start.1 = (bf16[1024,384]{1,0:T(8,128)(2,1)S(1)}, bf16[1024,384]{1,0:T(8,128)(2,1)}, u32[]{:S(2)}) copy-start(bf16[1024,384]{1,0:T(8,128)(2,1)} %get-tuple-element.69) | copy-start | bytes 2359300

commit v2 on v1

v2 whole, which is shorter than its diff:
```python
import functools

import jax
import jax.numpy as jnp
from jax import lax
from jax.experimental import pallas as pl
from jax.experimental.pallas import tpu as pltpu
from jax.sharding import PartitionSpec as P

L = 384
BLOCK = 128
EPN = 4
RIM = 64
NODES = 256
EDGES = 1024
ROWS = 16
TILE = 256
COLORS = 3
COLS = 128
SIDE = 4
DOM = 64
EPS = 1e-05
BF = jnp.bfloat16
F32 = jnp.float32
MESH = pl.DeviceIdType.MESH

GROUPS = (1536, 1280, 1536)
NODE_G, CONTACT_G, EDGE_G = 0, 1, 2

ORDERS = (("z", "x", "y"), ("x", "y", "z"), ("y", "z", "x"))
STRIDE = {"y": 16, "x": 4, "z": 1}
AXES = ("y", "x", "z")
N_CHUNK = 4
S_META, S_HALO, S_RIM, S_F1, S_F2, S_F2B, S_H, S_F3, S_B1, S_B1B, S_B2, S_B3, S_G = range(13)
R_META, R_HALO, R_RIM, R_F1, R_F2, R_F2B, R_H, R_F3, R_B1, R_B1B, R_B2, R_B3, R_G = (
    0, 1, 2, 3, 6, 9, 10, 14, 18, 26, 27, 28, 29
)
CHUNK = ROWS // N_CHUNK
HALF = BLOCK // 2


def mm(a, b):
    return lax.dot_general(a, b, (((1,), (0,)), ((), ())), preferred_element_type=F32)


def mm_nt(a, b):
    return lax.dot_general(a, b, (((1,), (1,)), ((), ())), preferred_element_type=F32)


def mm_tn(a, b):
    return lax.dot_general(a, b, (((0,), (0,)), ((), ())), preferred_element_type=F32)


def row_mean(v):
    return jnp.sum(v, axis=-1, keepdims=True) * (1.0 / L)


def norm(y):
    center = y - row_mean(y)
    scale = lax.rsqrt(row_mean(center * center) + EPS)
    return center * scale, scale


def norm_back(u, scale, g):
    return scale * (g - row_mean(g) - u * row_mean(g * u))


def silu_parts(z):
    s = jax.nn.sigmoid(z)
    return (z * s).astype(BF), s * (1.0 + z * (1.0 - s))


def body(
    x_ref, src_ref, ncot_ref, block_ref, host_ref, remote_ref,
    es_hbm, ecot_hbm, wei_hbm, weo_hbm, wni_hbm, wno_hbm, wci_hbm, wco_hbm,
    node_out_hbm, edge_out_hbm, node_grad_hbm, edge_grad_hbm, node_hbm, contact_hbm, edge_hbm,
    es, ecot, wei, weo, wni, wno, wci, wco,
    plane, hs, hr, sbuf, rbuf, dz_all, r2, r3, r3src,
    gsend, g1, g2src, g2, g3, gout, node_out, edge_out, node_grad, edge_grad,
    halo, rim_out, rim_in, xext, onehot,
    meta_v, meta_s, table_v, table_s,
    e_u, e_r, e_h, e_a, e_dy, e_dz, mesh_sum,
    c_x, c_u, c_r, c_h, c_a, c_dy, p_own, csum, dzown, tsum, nbuf, dcon, dmesh,
    local_sem, ss, rs,
):
    me = lax.axis_index("dom")
    coord = {"y": lax.div(me, 16), "x": lax.rem(lax.div(me, 4), 4), "z": lax.rem(me, 4)}

    def around(axis, off):
        return lax.rem(coord[axis] + off, SIDE)

    def peer(axis, off):
        return me + (around(axis, off) - coord[axis]) * STRIDE[axis]

    up, down = lax.rem(me + 1, DOM), lax.rem(me + DOM - 1, DOM)

    def remote(src, dst, to, at, dev):
        return pltpu.make_async_remote_copy(
            src_ref=src, dst_ref=dst, send_sem=ss.at[to], recv_sem=rs.at[at],
            device_id={"dom": dev}, device_id_type=MESH,
        )

    def arrived(ref, sem):
        remote(ref, ref, 0, sem, up).wait_recv()

    def sent(ref, sem):
        remote(ref, ref, sem, 0, up).wait_send()

    def send(*args):
        remote(*args).start()

    loads = [
        pltpu.make_async_copy(src, dst, local_sem.at[i])
        for i, (src, dst) in enumerate(
            [(wci_hbm, wci), (es_hbm, es), (wei_hbm, wei), (weo_hbm, weo), (wco_hbm, wco),
             (wni_hbm, wni), (wno_hbm, wno), (ecot_hbm, ecot)]
        )
    ]
    for load in loads:
        load.start()

    outs = []

    def write(src, dst, i):
        out = pltpu.make_async_copy(src, dst, local_sem.at[i])
        out.start()
        outs.append(out)

    barrier = pltpu.get_barrier_semaphore()
    for axis in AXES:
        for off in (1, 2, 3):
            pl.semaphore_signal(barrier, inc=1, device_id={"dom": peer(axis, off)}, device_id_type=MESH)
    pl.semaphore_signal(barrier, inc=1, device_id={"dom": up}, device_id_type=MESH)
    pl.semaphore_signal(barrier, inc=1, device_id={"dom": down}, device_id_type=MESH)

    x = x_ref[...]
    place = lax.broadcasted_iota(jnp.int32, (1, 128), 1)
    for c in range(ROWS):
        host = host_ref[c]
        at = {"y": lax.div(host, 16), "x": lax.rem(lax.div(host, 4), 4), "z": lax.rem(host, 4)}
        code = [((at[a3] * SIDE + at[a2]) * SIDE + at[a1]) * 2 + remote_ref[c] for a1, a2, a3 in ORDERS]
        line = jnp.where(place < 32, code[0], jnp.where(place < 64, code[1], code[2]))
        line = jnp.where(place < 96, line, block_ref[c])
        for i in range(3):
            meta_v[i, 0, c:c + 1] = line
    for k, (a1, a2, a3) in enumerate(ORDERS):
        own = (coord[a2] * SIDE + coord[a1]) * 2
        for b in range(2):
            plane[k, own + b] = x_ref[b * BLOCK:(b + 1) * BLOCK, k * COLS:(k + 1) * COLS]
    pl.semaphore_wait(barrier, 11)

    for k, (a1, a2, a3) in enumerate(ORDERS):
        own = (coord[a2] * SIDE + coord[a1]) * 2
        for off in (1, 2, 3):
            part = plane.at[k, pl.ds(own, 2)]
            send(part, part, S_F1, R_F1 + k, peer(a1, off))
    send(x_ref.at[pl.ds(NODES - RIM, RIM)], halo.at[0], S_HALO, R_HALO, up)
    send(x_ref.at[pl.ds(0, RIM)], halo.at[1], S_HALO, R_HALO, down)
    for i, axis in enumerate(AXES):
        for off in (1, 2, 3):
            send(meta_v.at[i, 0], meta_v.at[i, SIDE - off], S_META, R_META, peer(axis, off))

    lanes = lax.broadcasted_iota(jnp.int32, (BLOCK, L), 1)
    idx = jnp.concatenate([src_ref[...].astype(F32)] * 16, axis=0).T
    for j in range(EDGES // BLOCK):
        col = idx[:, j:j + 1].astype(jnp.int32)
        onehot[j * BLOCK:(j + 1) * BLOCK, :] = jnp.where(col == lanes, 1.0, 0.0).astype(BF)
    for k in range(COLORS):
        for j in range(SIDE):
            dz_all[k, j, ROWS] = jnp.zeros((BLOCK, COLS), BF)
    csum[...] = jnp.zeros_like(csum)
    dzown[...] = jnp.zeros_like(dzown)
    loads[0].wait()
    p_own[...] = mm(x, wci[0:L]).reshape(2, BLOCK, L)

    for k, (a1, a2, a3) in enumerate(ORDERS):
        arrived(plane.at[k, pl.ds(0, 6)], R_F1 + k)
        part = plane.at[k, pl.ds(coord[a2] * 8, 8)]
        send(part, part, S_F2, R_F2 + k, peer(a2, 1))
        send(part, part, S_F2, R_F2 + k, peer(a2, 3))

    arrived(halo, R_HALO)
    has_low = (me > 0).astype(F32)
    has_high = (me < DOM - 1).astype(F32)
    xext[0:RIM] = (halo[0].astype(F32) * has_low).astype(BF)
    xext[RIM:RIM + NODES] = x
    xext[RIM + NODES:] = (halo[1].astype(F32) * has_high).astype(BF)

    arrived(meta_v.at[:, pl.ds(1, 3)], R_META)
    mine = [coord[a3] * 32 for a1, a2, a3 in ORDERS]
    sought = lax.rem(place, 32) + jnp.where(place < 32, mine[0], jnp.where(place < 64, mine[1], mine[2]))
    wide = lax.broadcasted_iota(jnp.int32, (ROWS, 128), 1)
    for j in range(SIDE):
        asked = [meta_v[AXES.index(a3), j] for a1, a2, a3 in ORDERS]
        asked = jnp.where(wide < 32, asked[0], jnp.where(wide < 64, asked[1], asked[2]))
        first = second = jnp.full((1, 128), ROWS, jnp.int32)
        for c in reversed(range(ROWS)):
            hit = asked[c:c + 1] == sought
            second = jnp.where(hit, first, second)
            first = jnp.where(hit, c, first)
        table_v[2 * j:2 * j + 1] = first
        table_v[2 * j + 1:2 * j + 2] = second
    to_smem = [
        pltpu.make_async_copy(meta_v, meta_s, local_sem.at[8]),
        pltpu.make_async_copy(table_v, table_s, local_sem.at[9]),
    ]
    for copy in to_smem:
        copy.start()

    for load in loads[1:4]:
        load.wait()

    quarter = TILE // EPN
    fan = jnp.where(
        lax.div(lax.broadcasted_iota(jnp.int32, (TILE, quarter), 0), EPN)
        == lax.broadcasted_iota(jnp.int32, (TILE, quarter), 1), 1.0, 0.0,
    ).astype(BF)

    def edge_forward(t):
        rows = pl.ds(pl.multiple_of(t * TILE, TILE), TILE)
        nodes = pl.ds(pl.multiple_of(t * quarter, quarter), quarter)
        state = es[rows]
        src = mm(onehot[rows], xext[...]).astype(BF)
        tgt = mm(fan, x_ref[nodes]).astype(BF)
        z = mm(state, wei[0:L]) + mm(src, wei[L:2 * L]) + mm(tgt, wei[2 * L:])
        a, h = silu_parts(z)
        u, r = norm(mm(a, weo[...]))
        out = (state.astype(F32) + u).astype(BF)
        edge_out[rows] = out
        mesh_sum[nodes] = mm_tn(fan, out).astype(BF)
        e_a[rows] = a
        e_h[rows] = h
        e_u[rows] = u.astype(BF)
        e_r[rows] = r

    for k, (a1, a2, a3) in enumerate(ORDERS):
        arrived(plane.at[k, pl.ds(0, 16)], R_F2 + k)
        part = plane.at[k, pl.ds(around(a2, 3) * 8, 4)]
        send(part, part, S_F2B, R_F2B, peer(a2, 1))
        part = plane.at[k, pl.ds(around(a2, 1) * 8 + 4, 4)]
        send(part, part, S_F2B, R_F2B, peer(a2, 3))

    edge_forward(0)

    for copy in to_smem:
        copy.wait()
    arrived(plane.at[:, pl.ds(0, 8)], R_F2B)

    def request(k, j, c):
        code = meta_s[AXES.index(ORDERS[k][2]), j, c, k * 32]
        return lax.rem(code, 32), lax.div(code, 32)

    for q in range(N_CHUNK):
        for k, (a1, a2, a3) in enumerate(ORDERS):
            for c in range(CHUNK):
                slot, _ = request(k, 2, q * CHUNK + c)
                hs[k, 0, q * CHUNK + c] = plane[k, slot, 0:HALF]
                hs[k, 1, q * CHUNK + c] = plane[k, slot, HALF:]
            part = pl.ds(q * CHUNK, CHUNK)
            send(hs.at[k, 0, part], hr[q].at[k, 0], S_H, R_H + q, peer(a3, 3))
            send(hs.at[k, 1, part], hr[q].at[k, 1], S_H, R_H + q, peer(a3, 1))
    for q in range(N_CHUNK):
        arrived(hr[q], R_H + q)
        for k, (a1, a2, a3) in enumerate(ORDERS):
            for c in range(CHUNK):
                row = q * CHUNK + c
                slot, where = request(k, 3, row)
                own = where == coord[a3]
                sbuf[k, 0, row, 0:HALF] = jnp.where(own, plane[k, slot, 0:HALF], hr[q][k, 0, c])
                sbuf[k, 0, row, HALF:] = plane[k, slot, HALF:]
                slot, where = request(k, 1, row)
                own = where == coord[a3]
                sbuf[k, 1, row, 0:HALF] = plane[k, slot, 0:HALF]
                sbuf[k, 1, row, HALF:] = jnp.where(own, plane[k, slot, HALF:], hr[q][k, 1, c])
            part = pl.ds(q * CHUNK, CHUNK)
            send(sbuf.at[k, 0, part], rbuf[q].at[k, 1], S_F3, R_F3 + q, peer(a3, 3))
            send(sbuf.at[k, 1, part], rbuf[q].at[k, 2], S_F3, R_F3 + q, peer(a3, 1))
        for k in range(COLORS):
            for c in range(CHUNK):
                rbuf[q][k, 0, c] = plane[k, request(k, 0, q * CHUNK + c)[0]]
        if q < 3:
            edge_forward(q + 1)

    loads[4].wait()
    for q in range(N_CHUNK):
        arrived(rbuf[q].at[:, pl.ds(1, 2)], R_F3 + q)

        @pl.loop(0, CHUNK // 2)
        def _(p):
            parts, owns, weights = [], [], []
            for s in range(2):
                c = q * CHUNK + 2 * p + s
                cols = []
                for k, (a1, a2, a3) in enumerate(ORDERS):
                    away = lax.rem(request(k, 0, c)[1] - coord[a3] + SIDE, SIDE)
                    cols.append(jnp.concatenate([
                        rbuf[q][k, lax.div(away + 1, 2), 2 * p + s, 0:HALF],
                        rbuf[q][k, jnp.minimum(away, 2), 2 * p + s, HALF:],
                    ], axis=0))
                parts.append(jnp.concatenate(cols, axis=1))
                block = meta_s[0, 0, c, 96]
                owns.append(p_own[block])
                weights.append(block.astype(F32))
            rows = pl.ds(pl.multiple_of(q * CHUNK * BLOCK + p * TILE, TILE), TILE)
            remote_rows = jnp.concatenate(parts, axis=0)
            c_x[rows] = remote_rows
            z = mm(remote_rows, wci[L:]) + jnp.concatenate(owns, axis=0)
            a, h = silu_parts(z)
            u, r = norm(mm(a, wco[...]))
            c_a[rows] = a
            c_h[rows] = h
            message = u.astype(BF)
            c_u[rows] = message
            c_r[rows] = r
            message = message.astype(F32)
            for s in range(2):
                m = message[s * BLOCK:(s + 1) * BLOCK]
                csum[1] += m * weights[s]
                csum[0] += m * (1.0 - weights[s])

    loads[5].wait()
    loads[6].wait()
    nbuf[:, 0:L] = x
    nbuf[:, L:2 * L] = mesh_sum[...]
    nbuf[:, 2 * L:] = csum[...].reshape(NODES, L).astype(BF)
    a, h = silu_parts(mm(nbuf[...], wni[...]))
    u, r = norm(mm(a, wno[...]))
    node_out[...] = (x.astype(F32) + u).astype(BF)
    write(node_out, node_out_hbm, 13)
    write(edge_out, edge_out_hbm, 14)
    ncot = ncot_ref[...].astype(F32)
    n_dy = norm_back(u, r, ncot).astype(BF)
    n_dz = (mm_nt(n_dy, wno[...]) * h).astype(BF)
    dcon[...] = mm_nt(n_dz, wni[2 * L:]).astype(BF).reshape(2, BLOCK, L)

    @pl.loop(0, ROWS // 2)
    def _(t):
        rows = pl.ds(pl.multiple_of(t * TILE, TILE), TILE)
        blocks = [meta_s[0, 0, 2 * t + s, 96] for s in range(2)]
        g = jnp.concatenate([dcon[b] for b in blocks], axis=0).astype(F32)
        dy = norm_back(c_u[rows].astype(F32), c_r[rows], g).astype(BF)
        c_dy[rows] = dy
        dz = (mm_nt(dy, wco[...]) * c_h[rows]).astype(BF)
        for s in range(2):
            part = dz[s * BLOCK:(s + 1) * BLOCK]
            weight = blocks[s].astype(F32)
            dzown[1] += part.astype(F32) * weight
            dzown[0] += part.astype(F32) * (1.0 - weight)
            for k in range(COLORS):
                dz_all[k, 0, 2 * t + s] = part[:, k * COLS:(k + 1) * COLS]
        for k, (a1, a2, a3) in enumerate(ORDERS):
            pair = pl.ds(2 * t, 2)
            send(dz_all.at[k, 0, pair], dz_all.at[k, 3, pair], S_B1, R_B1 + t, peer(a3, 1))
            send(dz_all.at[k, 0, pair], dz_all.at[k, 1, pair], S_B1, R_B1 + t, peer(a3, 3))

    def put(group, row, value):
        value = value.astype(BF)
        for k in range(COLORS):
            gsend[group][k, row:row + L] = value[:, k * COLS:(k + 1) * COLS]

    def sums_1(n):
        size = GROUPS[n] // 4
        for k, (a1, a2, a3) in enumerate(ORDERS):
            for off in (2, 1, 3):
                send(
                    gsend[n].at[k, pl.ds(around(a3, off) * size, size)], g1[n].at[k, off - 1],
                    S_G + 6 * n + 0, R_G + 6 * n + 0, peer(a3, off),
                )

    def sums_2(n):
        size = GROUPS[n] // 4
        piece = size // 4
        arrived(g1[n], R_G + 6 * n)
        for k, (a1, a2, a3) in enumerate(ORDERS):
            @pl.loop(0, 4)
            def _(t):
                rows = pl.ds(pl.multiple_of(t * piece, 16), piece)
                total = gsend[n][k, pl.ds(pl.multiple_of(coord[a3] * size + t * piece, 16), piece)].astype(F32)
                for o in range(3):
                    total += g1[n][k, o, rows].astype(F32)
                g2src[n][k, t] = total.astype(BF)

            for off in (2, 1, 3):
                send(
                    g2src[n].at[k, around(a2, off)], g2[n].at[k, off - 1],
                    S_G + 6 * n + 1, R_G + 6 * n + 1, peer(a2, off),
                )

    def sums_3(n):
        arrived(g2[n], R_G + 6 * n + 1)
        for k, (a1, a2, a3) in enumerate(ORDERS):
            total = g2src[n][k, coord[a2]].astype(F32)
            for o in range(3):
                total += g2[n][k, o].astype(F32)
            g3[n][k, coord[a1]] = total.astype(BF)
            part = g3[n].at[k, coord[a1]]
            for off in (2, 1, 3):
                send(part, part, S_G + 6 * n + 2, R_G + 6 * n + 2, peer(a1, off))

    def sums_4(n):
        arrived(g2[n], R_G + 6 * n + 2)
        for k, (a1, a2, a3) in enumerate(ORDERS):
            total = g3[n][k, 0].astype(F32)
            for o in range(1, SIDE):
                total += g3[n][k, o].astype(F32)
            gout[n][k, coord[a3], coord[a2]] = total.astype(BF)
            part = gout[n].at[k, coord[a3], coord[a2]]
            for off in (2, 1, 3):
                send(part, part, S_G + 6 * n + 3, R_G + 6 * n + 3, peer(a2, off))

    def sums_5(n):
        arrived(g2[n], R_G + 6 * n + 3)
        for k, (a1, a2, a3) in enumerate(ORDERS):
            part = gout[n].at[k, coord[a3]]
            send(part, part, S_G + 6 * n + 4, R_G + 6 * n + 4, peer(a3, 1))
            send(part, part, S_G + 6 * n + 4, R_G + 6 * n + 4, peer(a3, 3))

    def sums_6(n):
        arrived(gout[n].at[:, pl.ds(0, 2)], R_G + 6 * n + 4)
        for k, (a1, a2, a3) in enumerate(ORDERS):
            part = gout[n].at[k, around(a3, 3), pl.ds(0, 2)]
            send(part, part, S_G + 6 * n + 5, R_G + 6 * n + 5, peer(a3, 1))
            part = gout[n].at[k, around(a3, 1), pl.ds(2, 2)]
            send(part, part, S_G + 6 * n + 5, R_G + 6 * n + 5, peer(a3, 3))

    def sums_7(n):
        arrived(gout[n].at[:, 0], R_G + 6 * n + 5)
        write(gout[n], (node_hbm, contact_hbm, edge_hbm)[n], 10 + n)

    for k in range(COLORS):
        gsend[CONTACT_G][k, 3 * L:] = jnp.zeros((GROUPS[CONTACT_G] - 3 * L, COLS), BF)
    put(NODE_G, 3 * L, mm_tn(a, n_dy))
    for i in range(3):
        put(NODE_G, i * L, mm_tn(nbuf[:, i * L:(i + 1) * L], n_dz))
    sums_1(NODE_G)
    own_low = dzown[...].reshape(NODES, L).astype(BF)
    put(CONTACT_G, 0, mm_tn(x, own_low))
    hidden = jnp.concatenate(
        [dz_all[k, 0, 0:ROWS].reshape(ROWS * BLOCK, COLS) for k in range(COLORS)], axis=1
    )
    put(CONTACT_G, L, mm_tn(c_x[...], hidden))
    put(CONTACT_G, 2 * L, mm_tn(c_a[...], c_dy[...]))
    sums_1(CONTACT_G)

    dmesh[...] = mm_nt(n_dz, wni[L:2 * L]).astype(BF)
    loads[7].wait()

    def edge_backward(t):
        rows = pl.ds(pl.multiple_of(t * TILE, TILE), TILE)
        nodes = pl.ds(pl.multiple_of(t * quarter, quarter), quarter)
        g = ecot[rows].astype(F32) + mm(fan, dmesh[nodes])
        dy = norm_back(e_u[rows].astype(F32), e_r[rows], g).astype(BF)
        dz = (mm_nt(dy, weo[...]) * e_h[rows]).astype(BF)
        edge_grad[rows] = (g + mm_nt(dz, wei[0:L])).astype(BF)
        tsum[nodes] = mm_tn(fan, dz).astype(BF)
        e_dy[rows] = dy
        e_dz[rows] = dz

    @pl.loop(0, 4)
    def _(t):
        edge_backward(t)
        for tile in (2 * t, 2 * t + 1):
            arrived(dz_all.at[:, pl.ds(0, 2), pl.ds(0, 2)], R_B1 + tile)
            for k, (a1, a2, a3) in enumerate(ORDERS):
                even, odd = pl.ds(2 * tile, 1), pl.ds(2 * tile + 1, 1)
                send(dz_all.at[k, 3, even], dz_all.at[k, 2, even], S_B1B, R_B1B, peer(a3, 1))
                send(dz_all.at[k, 1, odd], dz_all.at[k, 2, odd], S_B1B, R_B1B, peer(a3, 3))

    write(edge_grad, edge_grad_hbm, 15)
    spread = mm_tn(onehot[...], e_dz[...])
    spread_low = spread.astype(BF)
    rim_out[0] = spread_low[0:RIM]
    rim_out[1] = spread_low[RIM + NODES:]
    send(rim_out.at[0], rim_in.at[0], S_RIM, R_RIM, down)
    send(rim_out.at[1], rim_in.at[1], S_RIM, R_RIM, up)
    put(EDGE_G, L, mm_tn(xext[...], spread_low))
    put(EDGE_G, 0, mm_tn(es[...], e_dz[...]))
    put(EDGE_G, 2 * L, mm_tn(x, tsum[...]))
    put(EDGE_G, 3 * L, mm_tn(e_a[...], e_dy[...]))
    sums_1(EDGE_G)

    arrived(dz_all.at[:, 2, pl.ds(0, ROWS)], R_B1B)
    sent(plane.at[:, pl.ds(0, 16)], S_F2)
    sent(plane.at[:, pl.ds(0, 8)], S_F2B)
    sent(r3, S_F1)

    for off in (2, 1, 3, 0):
        group = [around(a2, off) * 8 for a1, a2, a3 in ORDERS]

        @pl.loop(0, 8)
        def _(s):
            for k in range(COLORS):
                total = jnp.zeros((BLOCK, COLS), F32)
                for j in range(SIDE):
                    for i in range(2):
                        total += dz_all[k, j, table_s[2 * j + i, k * 32 + group[k] + s]].astype(F32)
                plane[k, group[k] + s] = total.astype(BF)

        if off:
            for k, (a1, a2, a3) in enumerate(ORDERS):
                send(
                    plane.at[k, pl.ds(group[k], 8)], r2.at[k, off - 1],
                    S_B2, R_B2, peer(a2, off),
                )
    sums_2(NODE_G)
    sums_2(CONTACT_G)
    grad = ncot + mm_nt(n_dz, wni[0:L]) + mm_nt(tsum[...], wei[2 * L:]) + mm_nt(own_low, wci[0:L])

    arrived(r2, R_B2)
    for k, (a1, a2, a3) in enumerate(ORDERS):
        @pl.loop(0, 8)
        def _(s):
            total = plane[k, coord[a2] * 8 + s].astype(F32)
            for o in range(3):
                total += r2[k, o, s].astype(F32)
            r3src[k, s] = total.astype(BF)

        for off in (1, 2, 3):
            send(
                r3src.at[k, pl.ds(around(a1, off) * 2, 2)], r3.at[k, off - 1],
                S_B3, R_B3, peer(a1, off),
            )
    sums_3(NODE_G)
    sums_3(CONTACT_G)
    sums_2(EDGE_G)
    sums_4(NODE_G)
    sums_4(CONTACT_G)
    sums_3(EDGE_G)
    arrived(rim_in, R_RIM)
    first = spread[RIM:2 * RIM] + rim_in[1].astype(F32) * has_low
    last = spread[NODES:NODES + RIM] + rim_in[0].astype(F32) * has_high
    own_spread = jnp.concatenate([first, spread[2 * RIM:NODES], last], axis=0).astype(BF)
    grad += mm_nt(own_spread, wei[L:2 * L])
    arrived(r3, R_B3)
    cols = []
    for k, (a1, a2, a3) in enumerate(ORDERS):
        halves = [r3src[k, coord[a1] * 2 + b].astype(F32) for b in range(2)]
        for off in (1, 2, 3):
            halves = [halves[b] + r3[k, off - 1, b].astype(F32) for b in range(2)]
        cols.append(jnp.concatenate(halves, axis=0).astype(BF))
    s_rem = jnp.concatenate(cols, axis=1)
    node_grad[...] = (grad + mm_nt(s_rem, wci[L:])).astype(BF)
    write(node_grad, node_grad_hbm, 16)

    sums_5(NODE_G)
    sums_4(EDGE_G)
    sums_5(CONTACT_G)
    sums_6(NODE_G)
    sums_5(EDGE_G)
    sums_6(CONTACT_G)
    sums_7(NODE_G)
    sums_6(EDGE_G)
    sums_7(CONTACT_G)
    sums_7(EDGE_G)

    for ref, sem in (
        (meta_v.at[:, pl.ds(1, 3)], S_META), (halo, S_HALO), (rim_in, S_RIM), (hs, S_H), (sbuf, S_F3), (sbuf, S_B1),
        (dz_all.at[:, 2, pl.ds(0, ROWS)], S_B1B), (r2, S_B2), (r3, S_B3),
    ):
        sent(ref, sem)
    for n in range(3):
        refs = (g1[n], g2[n], g2[n], g2[n], gout[n].at[:, pl.ds(0, 2)], gout[n].at[:, 0])
        for i, ref in enumerate(refs):
            sent(ref, S_G + 6 * n + i)
    for out in outs:
        out.wait()


def dma(*shape):
    return pltpu.SemaphoreType.DMA(shape)


def vm(shape, dtype):
    return pltpu.VMEM(shape, dtype)


def fused(x, src, ncot, block, host, remote, es, ecot, wei, weo, wni, wno, wci, wco):
    tile = (BLOCK, COLS)
    pieces = [rows // 16 for rows in GROUPS]
    scratch = [
        vm((EDGES, L), BF), vm((EDGES, L), BF), vm((3 * L, L), BF), vm((L, L), BF), vm((3 * L, L), BF),
        vm((L, L), BF), vm((2 * L, L), BF), vm((L, L), BF),
        vm((COLORS, 32) + tile, BF),
        vm((COLORS, 2, ROWS, HALF, COLS), BF),
        [vm((COLORS, 2, CHUNK, HALF, COLS), BF) for _ in range(N_CHUNK)],
        vm((COLORS, 2, ROWS) + tile, BF),
        [vm((COLORS, 3, CHUNK) + tile, BF) for _ in range(N_CHUNK)],
        vm((COLORS, SIDE, ROWS + 1) + tile, BF),
        vm((COLORS, 3, 8) + tile, BF), vm((COLORS, 3, 2) + tile, BF), vm((COLORS, 8) + tile, BF),
        [vm((COLORS, rows, COLS), BF) for rows in GROUPS],
        [vm((COLORS, 3, rows // 4, COLS), BF) for rows in GROUPS],
        [vm((COLORS, SIDE, piece, COLS), BF) for piece in pieces],
        [vm((COLORS, 3, piece, COLS), BF) for piece in pieces],
        [vm((COLORS, SIDE, piece, COLS), BF) for piece in pieces],
        [vm((COLORS, SIDE, SIDE, piece, COLS), BF) for piece in pieces],
        vm((NODES, L), BF), vm((EDGES, L), BF), vm((NODES, L), BF), vm((EDGES, L), BF),
        vm((2, RIM, L), BF), vm((2, RIM, L), BF), vm((2, RIM, L), BF), vm((NODES + 2 * RIM, L), BF), vm((EDGES, L), BF),
        vm((3, SIDE, ROWS, 128), jnp.int32), pltpu.SMEM((3, SIDE, ROWS, 128), jnp.int32),
        vm((8, 128), jnp.int32), pltpu.SMEM((8, 128), jnp.int32),
        vm((EDGES, L), BF), vm((EDGES, 1), F32), vm((EDGES, L), F32), vm((EDGES, L), BF),
        vm((EDGES, L), BF), vm((EDGES, L), BF), vm((NODES, L), BF),
        vm((ROWS * BLOCK, L), BF), vm((ROWS * BLOCK, L), BF), vm((ROWS * BLOCK, 1), F32), vm((ROWS * BLOCK, L), F32),
        vm((ROWS * BLOCK, L), BF),
        vm((ROWS * BLOCK, L), BF), vm((2, BLOCK, L), F32), vm((2, BLOCK, L), F32), vm((2, BLOCK, L), F32),
        vm((NODES, L), BF), vm((NODES, 3 * L), BF), vm((2, BLOCK, L), BF), vm((NODES, L), BF),
        dma(17), dma(S_G + 18), dma(R_G + 18),
    ]
    here = pl.BlockSpec(memory_space=pltpu.VMEM)
    there = pl.BlockSpec(memory_space=pl.ANY)
    scalars = pl.BlockSpec(memory_space=pltpu.SMEM)
    return pl.pallas_call(
        body,
        out_shape=(
            jax.ShapeDtypeStruct((NODES, L), BF), jax.ShapeDtypeStruct((EDGES, L), BF),
            jax.ShapeDtypeStruct((NODES, L), BF), jax.ShapeDtypeStruct((EDGES, L), BF),
        ) + tuple(jax.ShapeDtypeStruct((COLORS, SIDE, SIDE, piece, COLS), BF) for piece in pieces),
        in_specs=[here] * 3 + [scalars] * 3 + [there] * 8,
        out_specs=[there] * 7,
        scratch_shapes=scratch,
        compiler_params=pltpu.CompilerParams(
            collective_id=0, has_side_effects=True, vmem_limit_bytes=63 * 1024 * 1024
        ),
        name="layer",
    )(x, src, ncot, block, host, remote, es, ecot, wei, weo, wni, wno, wci, wco)


def finish_body(*refs):
    plain_in, packed_in = refs[0:4], refs[4:7]
    plain_out, wide_out = refs[7:11], refs[11:17]
    plain, packed, wide, in_sem, out_sem = refs[17:21], refs[21:24], refs[24:27], refs[27], refs[28]
    loads = [pltpu.make_async_copy(packed_in[n], packed[n], in_sem.at[n]) for n in range(3)]
    loads += [pltpu.make_async_copy(plain_in[i], plain[i], in_sem.at[3 + i]) for i in range(4)]
    for load in loads:
        load.start()
    stores = []

    def store(src, dst):
        copy = pltpu.make_async_copy(src, dst, out_sem.at[len(stores)])
        copy.start()
        stores.append(copy)

    for n, first in enumerate((3 * L, 2 * L, 3 * L)):
        loads[n].wait()
        for k in range(COLORS):
            wide[n][:, k * COLS:(k + 1) * COLS] = packed[n][k].astype(F32)
        store(wide[n].at[pl.ds(0, first)], wide_out[2 * n])
        store(wide[n].at[pl.ds(first, L)], wide_out[2 * n + 1])
    for i in range(4):
        loads[3 + i].wait()
        store(plain[i], plain_out[i])
    for copy in stores:
        copy.wait()


def finish(plain, packed):
    packed = [p.reshape(COLORS, rows, COLS) for p, rows in zip(packed, GROUPS)]
    there = pl.BlockSpec(memory_space=pl.ANY)
    shapes = [jax.ShapeDtypeStruct(p.shape, p.dtype) for p in plain]
    shapes += [jax.ShapeDtypeStruct((n * L, L), F32) for n in (3, 1, 2, 1, 3, 1)]
    return pl.pallas_call(
        finish_body,
        out_shape=shapes,
        in_specs=[there] * 7,
        out_specs=[there] * 10,
        scratch_shapes=[
            *[vm(p.shape, p.dtype) for p in plain],
            *[vm((COLORS, rows, COLS), BF) for rows in GROUPS],
            *[vm((rows, L), F32) for rows in GROUPS],
            dma(7), dma(10),
        ],
        compiler_params=pltpu.CompilerParams(vmem_limit_bytes=63 * 1024 * 1024),
        name="finish",
    )(*plain, *packed)


def on_device(
    node_state, edge_state, edge_source, contact_block, contact_host, contact_remote,
    w_edge_in, w_edge_out, w_node_in, w_node_out, w_contact_in, w_contact_out, node_cot, edge_cot,
):
    results = fused(
        node_state, edge_source.reshape(8, 128), node_cot, contact_block, contact_host.reshape(ROWS), contact_remote,
        edge_state, edge_cot, w_edge_in, w_edge_out, w_node_in, w_node_out, w_contact_in, w_contact_out,
    )
    out = finish(results[:4], results[4:])
    node_in, node_last, contact_in, contact_last, edge_in, edge_last = out[4:]
    return tuple(out[:4]) + (edge_in, edge_last, node_in, node_last, contact_in, contact_last)


def solution(mesh):
    rows = P(("rep", "dom"), None)
    flat = P(("rep", "dom"))
    weight = P("rep", None)
    return jax.shard_map(
        on_device,
        mesh=mesh,
        in_specs=(rows, rows, flat, flat, rows, flat) + (weight,) * 6 + (rows, rows),
        out_specs=(rows,) * 4 + (weight,) * 6,
        check_vma=False,
    )
```

time: 155 us -> 127 us (0.82)
  Pallas kernels: 140 us -> 126 us
  other arithmetic: 7.77 us -> 0 us
  local copies, waits for them, and re-layouts: 6.99 us -> 0 us
    pallas_call x1, Pallas kernels: 140 us -> 121 us  [fused(): pl.pallas_call(body, out_shape=(jax.ShapeDtypeStruct((NODES, L), BF), jax...]
    convert_element_type x4 -> x0, other arithmetic: 5.05 us -> none  [grad(): jnp.concatenate([packed[k, row:row + count] for k in range(COLORS)], axis=1)]
    pallas_call x0 -> x1, Pallas kernels: none -> 4.93 us  [finish(): pl.pallas_call(finish_body, out_shape=shapes, in_specs=[there] * 7, out_s...]
    unnamed x14 -> x0, local copies, waits for them, and re-layouts: 3.13 us -> none
    squeeze x3 -> x0, local copies, waits for them, and re-layouts: 2.89 us -> none  [grad(): packed[k, row:row + count]]
where the time goes in v2:
time: 127 us
  Pallas kernels  126 us (99%)
    pallas_call x1, Pallas kernels, fused(): pl.pallas_call(body, out_shape=(jax.ShapeDtypeStruct((NODES, L), BF), jax...  121 us
    pallas_call x1, Pallas kernels, finish(): pl.pallas_call(finish_body, out_shape=shapes, in_specs=[there] * 7, out_s...  4.93 us

profile of v2, /device:TPU:0, one launch (start us, length us, event | category | flops | bytes accessed | tf_op | source)
XLA Modules:
  0.0 126.9 jit_solution(8655967792885036384)
XLA Ops:
  0.6 121.1 %layer.1 = (bf16[256,384]{1,0:T(8,128)(2,1)}, bf16[1024,384]{1,0:T(8,128)(2,1)}, bf16[256,384]{1,0:T(8,128)(2,1)}, bf16[1024,384]{1,0:T(8,128)(2,1)}, bf16[3,4,4...) custom-call(bf16[256,384]{1,0:T(8,128)(2,1)} %x_ref.1, ...), custom_call_target="tpu_custom_call" | custom-call | tf_op jit(solution)/shard_map/layer/pallas_call | solution.py:611
  121.8 4.9 %finish.1 = (bf16[256,384]{1,0:T(8,128)(2,1)}, bf16[1024,384]{1,0:T(8,128)(2,1)}, bf16[256,384]{1,0:T(8,128)(2,1)}, bf16[1024,384]{1,0:T(8,128)(2,1)}, f32[1152,...) custom-call(bf16[256,384]{1,0:T(8,128)(2,1)} %get-tuple-element.27.r, ...), custom_call_target="tpu_custom_call" | custom-call | tf_op jit(solution)/shard_map/finish/pallas_call | solution.py:660

commit v3 on v2

--- a/solution.py
+++ b/solution.py
@@ -31,9 +31,9 @@
 STRIDE = {"y": 16, "x": 4, "z": 1}
 AXES = ("y", "x", "z")
 N_CHUNK = 4
-S_META, S_HALO, S_RIM, S_F1, S_F2, S_F2B, S_H, S_F3, S_B1, S_B1B, S_B2, S_B3, S_G = range(13)
-R_META, R_HALO, R_RIM, R_F1, R_F2, R_F2B, R_H, R_F3, R_B1, R_B1B, R_B2, R_B3, R_G = (
-    0, 1, 2, 3, 6, 9, 10, 14, 18, 26, 27, 28, 29
+S_META, S_HALO, S_RIM, S_F1, S_F2, S_F2B, S_H, S_F3, S_B1, S_B1B, S_B2H, S_B2, S_B3, S_G = range(14)
+R_META, R_HALO, R_RIM, R_F1, R_F2, R_F2B, R_H, R_F3, R_B1, R_B1B, R_B2H, R_B2, R_B3, R_G = (
+    0, 1, 2, 3, 6, 9, 10, 14, 18, 26, 27, 28, 29, 30
 )
 CHUNK = ROWS // N_CHUNK
 HALF = BLOCK // 2
@@ -75,8 +75,8 @@
     es_hbm, ecot_hbm, wei_hbm, weo_hbm, wni_hbm, wno_hbm, wci_hbm, wco_hbm,
     node_out_hbm, edge_out_hbm, node_grad_hbm, edge_grad_hbm, node_hbm, contact_hbm, edge_hbm,
     es, ecot, wei, weo, wni, wno, wci, wco,
-    plane, hs, hr, sbuf, rbuf, dz_all, r2, r3, r3src,
-    gsend, g1, g2src, g2, g3, gout, node_out, edge_out, node_grad, edge_grad,
+    plane, hs, hr, sbuf, rbuf, dz_all, r2h, r2, r3, r3src,
+    gsend, g1h, g1, g2src, g2, g3, gout, node_out, edge_out, node_grad, edge_grad,
     halo, rim_out, rim_in, xext, onehot,
     meta_v, meta_s, table_v, table_s,
     e_u, e_r, e_h, e_a, e_dy, e_dz, mesh_sum,
@@ -326,8 +326,8 @@
     a, h = silu_parts(mm(nbuf[...], wni[...]))
     u, r = norm(mm(a, wno[...]))
     node_out[...] = (x.astype(F32) + u).astype(BF)
-    write(node_out, node_out_hbm, 13)
-    write(edge_out, edge_out_hbm, 14)
+    write(node_out, node_out_hbm, 10)
+    write(edge_out, edge_out_hbm, 11)
     ncot = ncot_ref[...].astype(F32)
     n_dy = norm_back(u, r, ncot).astype(BF)
     n_dz = (mm_nt(n_dy, wno[...]) * h).astype(BF)
@@ -360,34 +360,48 @@
 
     def sums_1(n):
         size = GROUPS[n] // 4
-        for k, (a1, a2, a3) in enumerate(ORDERS):
-            for off in (2, 1, 3):
+        half = size // 2
+        for k, (a1, a2, a3) in enumerate(ORDERS):
+            far = around(a3, 2) * size
+            send(gsend[n].at[k, pl.ds(far, half)], g1h[n].at[k, 0], S_G + 7 * n, R_G + 7 * n, peer(a3, 1))
+            send(gsend[n].at[k, pl.ds(far + half, half)], g1h[n].at[k, 1], S_G + 7 * n, R_G + 7 * n, peer(a3, 3))
+
+    def sums_1b(n):
+        size = GROUPS[n] // 4
+        half = size // 2
+        arrived(g1h[n], R_G + 7 * n)
+        for k, (a1, a2, a3) in enumerate(ORDERS):
+            for i, off in enumerate((1, 3)):
+                start = around(a3, off) * size
+                rows = pl.ds(pl.multiple_of(start + i * half, 16), half)
+                total = gsend[n][k, rows].astype(F32) + g1h[n][k, i].astype(F32)
+                gsend[n][k, rows] = total.astype(BF)
                 send(
-                    gsend[n].at[k, pl.ds(around(a3, off) * size, size)], g1[n].at[k, off - 1],
-                    S_G + 6 * n + 0, R_G + 6 * n + 0, peer(a3, off),
+                    gsend[n].at[k, pl.ds(start, size)], g1[n].at[k, i],
+                    S_G + 7 * n + 1, R_G + 7 * n + 1, peer(a3, off),
                 )
 
     def sums_2(n):
         size = GROUPS[n] // 4
         piece = size // 4
-        arrived(g1[n], R_G + 6 * n)
+        arrived(g1[n], R_G + 7 * n + 1)
         for k, (a1, a2, a3) in enumerate(ORDERS):
             @pl.loop(0, 4)
             def _(t):
                 rows = pl.ds(pl.multiple_of(t * piece, 16), piece)
                 total = gsend[n][k, pl.ds(pl.multiple_of(coord[a3] * size + t * piece, 16), piece)].astype(F32)
-                for o in range(3):
+                for o in range(2):
                     total += g1[n][k, o, rows].astype(F32)
                 g2src[n][k, t] = total.astype(BF)
 
             for off in (2, 1, 3):
                 send(
                     g2src[n].at[k, around(a2, off)], g2[n].at[k, off - 1],
-                    S_G + 6 * n + 1, R_G + 6 * n + 1, peer(a2, off),
+                    S_G + 7 * n + 2, R_G + 7 * n + 2, peer(a2, off),
                 )
 
     def sums_3(n):
-        arrived(g2[n], R_G + 6 * n + 1)
+        arrived(g2[n], R_G + 7 * n + 2)
         for k, (a1, a2, a3) in enumerate(ORDERS):
             total = g2src[n][k, coord[a2]].astype(F32)
             for o in range(3):
@@ -395,10 +409,10 @@
             g3[n][k, coord[a1]] = total.astype(BF)
             part = g3[n].at[k, coord[a1]]
             for off in (2, 1, 3):
-                send(part, part, S_G + 6 * n + 2, R_G + 6 * n + 2, peer(a1, off))
+                send(part, part, S_G + 7 * n + 3, R_G + 7 * n + 3, peer(a1, off))
 
     def sums_4(n):
-        arrived(g2[n], R_G + 6 * n + 2)
+        arrived(g2[n], R_G + 7 * n + 3)
         for k, (a1, a2, a3) in enumerate(ORDERS):
             total = g3[n][k, 0].astype(F32)
             for o in range(1, SIDE):
@@ -406,26 +420,33 @@
             gout[n][k, coord[a3], coord[a2]] = total.astype(BF)
             part = gout[n].at[k, coord[a3], coord[a2]]
             for off in (2, 1, 3):
-                send(part, part, S_G + 6 * n + 3, R_G + 6 * n + 3, peer(a2, off))
+                send(part, part, S_G + 7 * n + 4, R_G + 7 * n + 4, peer(a2, off))
 
     def sums_5(n):
-        arrived(g2[n], R_G + 6 * n + 3)
+        arrived(g2[n], R_G + 7 * n + 4)
         for k, (a1, a2, a3) in enumerate(ORDERS):
             part = gout[n].at[k, coord[a3]]
-            send(part, part, S_G + 6 * n + 4, R_G + 6 * n + 4, peer(a3, 1))
-            send(part, part, S_G + 6 * n + 4, R_G + 6 * n + 4, peer(a3, 3))
+            send(part, part, S_G + 7 * n + 5, R_G + 7 * n + 5, peer(a3, 1))
+            send(part, part, S_G + 7 * n + 5, R_G + 7 * n + 5, peer(a3, 3))
+
+    def keep(n, off):
+        for k, (a1, a2, a3) in enumerate(ORDERS):
+            at = around(a3, off)
+            write(gout[n].at[k, at], (node_hbm, contact_hbm, edge_hbm)[n].at[k, at], 14 + (n * 3 + k) * 4 + off)
 
     def sums_6(n):
-        arrived(gout[n].at[:, pl.ds(0, 2)], R_G + 6 * n + 4)
+        arrived(gout[n].at[:, pl.ds(0, 2)], R_G + 7 * n + 5)
         for k, (a1, a2, a3) in enumerate(ORDERS):
             part = gout[n].at[k, around(a3, 3), pl.ds(0, 2)]
-            send(part, part, S_G + 6 * n + 5, R_G + 6 * n + 5, peer(a3, 1))
+            send(part, part, S_G + 7 * n + 6, R_G + 7 * n + 6, peer(a3, 1))
             part = gout[n].at[k, around(a3, 1), pl.ds(2, 2)]
-            send(part, part, S_G + 6 * n + 5, R_G + 6 * n + 5, peer(a3, 3))
+            send(part, part, S_G + 7 * n + 6, R_G + 7 * n + 6, peer(a3, 3))
+        for off in (0, 1, 3):
+            keep(n, off)
 
     def sums_7(n):
-        arrived(gout[n].at[:, 0], R_G + 6 * n + 5)
-        write(gout[n], (node_hbm, contact_hbm, edge_hbm)[n], 10 + n)
+        arrived(gout[n].at[:, 0], R_G + 7 * n + 6)
+        keep(n, 2)
 
     for k in range(COLORS):
         gsend[CONTACT_G][k, 3 * L:] = jnp.zeros((GROUPS[CONTACT_G] - 3 * L, COLS), BF)
@@ -441,6 +462,7 @@
     put(CONTACT_G, L, mm_tn(c_x[...], hidden))
     put(CONTACT_G, 2 * L, mm_tn(c_a[...], c_dy[...]))
     sums_1(CONTACT_G)
+    sums_1b(NODE_G)
 
     dmesh[...] = mm_nt(n_dz, wni[L:2 * L]).astype(BF)
     loads[7].wait()
@@ -456,54 +478,91 @@
         e_dy[rows] = dy
         e_dz[rows] = dz
 
+    def pass_on(tile):
+        arrived(dz_all.at[:, pl.ds(0, 2), pl.ds(0, 2)], R_B1 + tile)
+        for k, (a1, a2, a3) in enumerate(ORDERS):
+            even, odd = pl.ds(2 * tile, 1), pl.ds(2 * tile + 1, 1)
+            send(dz_all.at[k, 3, even], dz_all.at[k, 2, even], S_B1B, R_B1B, peer(a3, 1))
+            send(dz_all.at[k, 1, odd], dz_all.at[k, 2, odd], S_B1B, R_B1B, peer(a3, 3))
+
     @pl.loop(0, 4)
     def _(t):
         edge_backward(t)
-        for tile in (2 * t, 2 * t + 1):
-            arrived(dz_all.at[:, pl.ds(0, 2), pl.ds(0, 2)], R_B1 + tile)
-            for k, (a1, a2, a3) in enumerate(ORDERS):
-                even, odd = pl.ds(2 * tile, 1), pl.ds(2 * tile + 1, 1)
-                send(dz_all.at[k, 3, even], dz_all.at[k, 2, even], S_B1B, R_B1B, peer(a3, 1))
-                send(dz_all.at[k, 1, odd], dz_all.at[k, 2, odd], S_B1B, R_B1B, peer(a3, 3))
-
-    write(edge_grad, edge_grad_hbm, 15)
+
+        @pl.when(t > 0)
+        def _():
+            pass_on(2 * t - 1)
+
+        pass_on(2 * t)
+
+    write(edge_grad, edge_grad_hbm, 12)
+    sums_1b(CONTACT_G)
     spread = mm_tn(onehot[...], e_dz[...])
     spread_low = spread.astype(BF)
     rim_out[0] = spread_low[0:RIM]
     rim_out[1] = spread_low[RIM + NODES:]
     send(rim_out.at[0], rim_in.at[0], S_RIM, R_RIM, down)
     send(rim_out.at[1], rim_in.at[1], S_RIM, R_RIM, up)
+    pass_on(7)
     put(EDGE_G, L, mm_tn(xext[...], spread_low))
     put(EDGE_G, 0, mm_tn(es[...], e_dz[...]))
     put(EDGE_G, 2 * L, mm_tn(x, tsum[...]))
     put(EDGE_G, 3 * L, mm_tn(e_a[...], e_dy[...]))
     sums_1(EDGE_G)
+    sums_2(NODE_G)
 
     arrived(dz_all.at[:, 2, pl.ds(0, ROWS)], R_B1B)
     sent(plane.at[:, pl.ds(0, 16)], S_F2)
     sent(plane.at[:, pl.ds(0, 8)], S_F2B)
     sent(r3, S_F1)
 
-    for off in (2, 1, 3, 0):
-        group = [around(a2, off) * 8 for a1, a2, a3 in ORDERS]
-
-        @pl.loop(0, 8)
-        def _(s):
-            for k in range(COLORS):
-                total = jnp.zeros((BLOCK, COLS), F32)
-                for j in range(SIDE):
-                    for i in range(2):
-                        total += dz_all[k, j, table_s[2 * j + i, k * 32 + group[k] + s]].astype(F32)
-                plane[k, group[k] + s] = total.astype(BF)
-
-        if off:
-            for k, (a1, a2, a3) in enumerate(ORDERS):
-                send(
-                    plane.at[k, pl.ds(group[k], 8)], r2.at[k, off - 1],
-                    S_B2, R_B2, peer(a2, off),
-                )
-    sums_2(NODE_G)
+    def slot_sum(k, s):
+        total = jnp.zeros((BLOCK, COLS), F32)
+        for j in range(SIDE):
+            for i in range(2):
+                total += dz_all[k, j, table_s[2 * j + i, k * 32 + s]].astype(F32)
+        return total
+
+    own, near, far, last = [[around(a2, off) * 8 for a1, a2, a3 in ORDERS] for off in range(4)]
+
+    @pl.loop(0, 8)
+    def _(s):
+        for k in range(COLORS):
+            plane[k, far[k] + s] = slot_sum(k, far[k] + s).astype(BF)
+
+    for k, (a1, a2, a3) in enumerate(ORDERS):
+        send(plane.at[k, pl.ds(far[k], 4)], r2h.at[k, 0], S_B2H, R_B2H, peer(a2, 1))
+        send(plane.at[k, pl.ds(far[k] + 4, 4)], r2h.at[k, 1], S_B2H, R_B2H, peer(a2, 3))
+    sums_1b(EDGE_G)
     sums_2(CONTACT_G)
+
+    @pl.loop(0, 4)
+    def _(s):
+        for k in range(COLORS):
+            plane[k, near[k] + 4 + s] = slot_sum(k, near[k] + 4 + s).astype(BF)
+            plane[k, last[k] + s] = slot_sum(k, last[k] + s).astype(BF)
+
+    arrived(r2h, R_B2H)
+
+    @pl.loop(0, 4)
+    def _(s):
+        for k in range(COLORS):
+            plane[k, near[k] + s] = (slot_sum(k, near[k] + s) + r2h[k, 0, s].astype(F32)).astype(BF)
+            plane[k, last[k] + 4 + s] = (slot_sum(k, last[k] + 4 + s) + r2h[k, 1, s].astype(F32)).astype(BF)
+
+    for k, (a1, a2, a3) in enumerate(ORDERS):
+        send(plane.at[k, pl.ds(near[k], 8)], r2.at[k, 0], S_B2, R_B2, peer(a2, 1))
+        send(plane.at[k, pl.ds(last[k], 8)], r2.at[k, 1], S_B2, R_B2, peer(a2, 3))
+    sums_3(NODE_G)
+
+    @pl.loop(0, 8)
+    def _(s):
+        for k in range(COLORS):
+            plane[k, own[k] + s] = slot_sum(k, own[k] + s).astype(BF)
+
+    sums_2(EDGE_G)
+    sums_4(NODE_G)
+    sums_3(CONTACT_G)
     grad = ncot + mm_nt(n_dz, wni[0:L]) + mm_nt(tsum[...], wei[2 * L:]) + mm_nt(own_low, wci[0:L])
 
     arrived(r2, R_B2)
@@ -511,7 +570,7 @@
         @pl.loop(0, 8)
         def _(s):
             total = plane[k, coord[a2] * 8 + s].astype(F32)
-            for o in range(3):
+            for o in range(2):
                 total += r2[k, o, s].astype(F32)
             r3src[k, s] = total.astype(BF)
 
@@ -520,12 +579,9 @@
                 r3src.at[k, pl.ds(around(a1, off) * 2, 2)], r3.at[k, off - 1],
                 S_B3, R_B3, peer(a1, off),
             )
-    sums_3(NODE_G)
-    sums_3(CONTACT_G)
-    sums_2(EDGE_G)
-    sums_4(NODE_G)
+    sums_3(EDGE_G)
+    sums_5(NODE_G)
     sums_4(CONTACT_G)
-    sums_3(EDGE_G)
     arrived(rim_in, R_RIM)
     first = spread[RIM:2 * RIM] + rim_in[1].astype(F32) * has_low
     last = spread[NODES:NODES + RIM] + rim_in[0].astype(F32) * has_high
@@ -540,12 +596,11 @@
         cols.append(jnp.concatenate(halves, axis=0).astype(BF))
     s_rem = jnp.concatenate(cols, axis=1)
     node_grad[...] = (grad + mm_nt(s_rem, wci[L:])).astype(BF)
-    write(node_grad, node_grad_hbm, 16)
-
-    sums_5(NODE_G)
+    write(node_grad, node_grad_hbm, 13)
+
     sums_4(EDGE_G)
+    sums_6(NODE_G)
     sums_5(CONTACT_G)
-    sums_6(NODE_G)
     sums_5(EDGE_G)
     sums_6(CONTACT_G)
     sums_7(NODE_G)
@@ -555,13 +610,13 @@
 
     for ref, sem in (
         (meta_v.at[:, pl.ds(1, 3)], S_META), (halo, S_HALO), (rim_in, S_RIM), (hs, S_H), (sbuf, S_F3), (sbuf, S_B1),
-        (dz_all.at[:, 2, pl.ds(0, ROWS)], S_B1B), (r2, S_B2), (r3, S_B3),
+        (dz_all.at[:, 2, pl.ds(0, ROWS)], S_B1B), (r2h, S_B2H), (r2, S_B2), (r3, S_B3),
     ):
         sent(ref, sem)
     for n in range(3):
-        refs = (g1[n], g2[n], g2[n], g2[n], gout[n].at[:, pl.ds(0, 2)], gout[n].at[:, 0])
+        refs = (g1h[n], g1[n], g2[n], g2[n], g2[n], gout[n].at[:, pl.ds(0, 2)], gout[n].at[:, 0])
         for i, ref in enumerate(refs):
-            sent(ref, S_G + 6 * n + i)
+            sent(ref, S_G + 7 * n + i)
     for out in outs:
         out.wait()
 
@@ -586,9 +641,10 @@
         vm((COLORS, 2, ROWS) + tile, BF),
         [vm((COLORS, 3, CHUNK) + tile, BF) for _ in range(N_CHUNK)],
         vm((COLORS, SIDE, ROWS + 1) + tile, BF),
-        vm((COLORS, 3, 8) + tile, BF), vm((COLORS, 3, 2) + tile, BF), vm((COLORS, 8) + tile, BF),
+        vm((COLORS, 2, 4) + tile, BF), vm((COLORS, 2, 8) + tile, BF), vm((COLORS, 3, 2) + tile, BF), vm((COLORS, 8) + tile, BF),
         [vm((COLORS, rows, COLS), BF) for rows in GROUPS],
-        [vm((COLORS, 3, rows // 4, COLS), BF) for rows in GROUPS],
+        [vm((COLORS, 2, rows // 8, COLS), BF) for rows in GROUPS],
+        [vm((COLORS, 2, rows // 4, COLS), BF) for rows in GROUPS],
         [vm((COLORS, SIDE, piece, COLS), BF) for piece in pieces],
         [vm((COLORS, 3, piece, COLS), BF) for piece in pieces],
         [vm((COLORS, SIDE, piece, COLS), BF) for piece in pieces],
@@ -603,7 +659,7 @@
         vm((ROWS * BLOCK, L), BF),
         vm((ROWS * BLOCK, L), BF), vm((2, BLOCK, L), F32), vm((2, BLOCK, L), F32), vm((2, BLOCK, L), F32),
         vm((NODES, L), BF), vm((NODES, 3 * L), BF), vm((2, BLOCK, L), BF), vm((NODES, L), BF),
-        dma(17), dma(S_G + 18), dma(R_G + 18),
+        dma(50), dma(S_G + 21), dma(R_G + 21),
     ]
     here = pl.BlockSpec(memory_space=pltpu.VMEM)
     there = pl.BlockSpec(memory_space=pl.ANY)
@@ -628,8 +684,14 @@
     plain_in, packed_in = refs[0:4], refs[4:7]
     plain_out, wide_out = refs[7:11], refs[11:17]
     plain, packed, wide, in_sem, out_sem = refs[17:21], refs[21:24], refs[24:27], refs[27], refs[28]
-    loads = [pltpu.make_async_copy(packed_in[n], packed[n], in_sem.at[n]) for n in range(3)]
-    loads += [pltpu.make_async_copy(plain_in[i], plain[i], in_sem.at[3 + i]) for i in range(4)]
+    chunks = []
+    for n, count in enumerate((3, 2, 3)):
+        chunks += [(n, i * L, 2 * n + i // count, i % count * L) for i in range(count + 1)]
+    loads = [
+        pltpu.make_async_copy(packed_in[n].at[:, pl.ds(row, L)], packed[n].at[:, pl.ds(row, L)], in_sem.at[i])
+        for i, (n, row, _, _) in enumerate(chunks)
+    ]
+    loads += [pltpu.make_async_copy(plain_in[i], plain[i], in_sem.at[len(chunks) + i]) for i in range(4)]
     for load in loads:
         load.start()
     stores = []
@@ -639,14 +701,13 @@
         copy.start()
         stores.append(copy)
 
-    for n, first in enumerate((3 * L, 2 * L, 3 * L)):
-        loads[n].wait()
+    for i, (n, row, which, there) in enumerate(chunks):
+        loads[i].wait()
         for k in range(COLORS):
-            wide[n][:, k * COLS:(k + 1) * COLS] = packed[n][k].astype(F32)
-        store(wide[n].at[pl.ds(0, first)], wide_out[2 * n])
-        store(wide[n].at[pl.ds(first, L)], wide_out[2 * n + 1])
+            wide[n][row:row + L, k * COLS:(k + 1) * COLS] = packed[n][k, row:row + L].astype(F32)
+        store(wide[n].at[pl.ds(row, L)], wide_out[which].at[pl.ds(there, L)])
     for i in range(4):
-        loads[3 + i].wait()
+        loads[len(chunks) + i].wait()
         store(plain[i], plain_out[i])
     for copy in stores:
         copy.wait()
@@ -666,7 +727,7 @@
             *[vm(p.shape, p.dtype) for p in plain],
             *[vm((COLORS, rows, COLS), BF) for rows in GROUPS],
             *[vm((rows, L), F32) for rows in GROUPS],
-            dma(7), dma(10),
+            dma(15), dma(15),
         ],
         compiler_params=pltpu.CompilerParams(vmem_limit_bytes=63 * 1024 * 1024),
         name="finish",

time: 127 us -> 122 us (0.961)
  Pallas kernels: 126 us -> 121 us
    pallas_call x1, Pallas kernels: 121 us -> 116 us  [fused(): pl.pallas_call(body, out_shape=(jax.ShapeDtypeStruct((NODES, L), BF), jax...]
where the time goes in v3:
time: 122 us
  Pallas kernels  121 us (99%)
    pallas_call x1, Pallas kernels, fused(): pl.pallas_call(body, out_shape=(jax.ShapeDtypeStruct((NODES, L), BF), jax...  116 us
    pallas_call x1, Pallas kernels, finish(): pl.pallas_call(finish_body, out_shape=shapes, in_specs=[there] * 7, out_s...  4.98 us

profile of v3, /device:TPU:0, one launch (start us, length us, event | category | flops | bytes accessed | tf_op | source)
XLA Modules:
  0.0 121.7 jit_solution(6559799716237267511)
XLA Ops:
  0.6 115.9 %layer.1 = (bf16[256,384]{1,0:T(8,128)(2,1)}, bf16[1024,384]{1,0:T(8,128)(2,1)}, bf16[256,384]{1,0:T(8,128)(2,1)}, bf16[1024,384]{1,0:T(8,128)(2,1)}, bf16[3,4,4...) custom-call(bf16[256,384]{1,0:T(8,128)(2,1)} %x_ref.1, ...), custom_call_target="tpu_custom_call" | custom-call | tf_op jit(solution)/shard_map/layer/pallas_call | solution.py:667
  116.5 5.0 %finish.1 = (bf16[256,384]{1,0:T(8,128)(2,1)}, bf16[1024,384]{1,0:T(8,128)(2,1)}, bf16[256,384]{1,0:T(8,128)(2,1)}, bf16[1024,384]{1,0:T(8,128)(2,1)}, f32[1152,...) custom-call(bf16[256,384]{1,0:T(8,128)(2,1)} %get-tuple-element.27.r, ...), custom_call_target="tpu_custom_call" | custom-call | tf_op jit(solution)/shard_map/finish/pallas_call | solution.py:721

commit v4 on v3

--- a/solution.py
+++ b/solution.py
@@ -75,7 +75,7 @@
     es_hbm, ecot_hbm, wei_hbm, weo_hbm, wni_hbm, wno_hbm, wci_hbm, wco_hbm,
     node_out_hbm, edge_out_hbm, node_grad_hbm, edge_grad_hbm, node_hbm, contact_hbm, edge_hbm,
     es, ecot, wei, weo, wni, wno, wci, wco,
-    plane, hs, hr, sbuf, rbuf, dz_all, r2h, r2, r3, r3src,
+    plane, hs, hr, sbuf, rbuf, dz_near, dz_far, r2h, r2, r3, r3src,
     gsend, g1h, g1, g2src, g2, g3, gout, node_out, edge_out, node_grad, edge_grad,
     halo, rim_out, rim_in, xext, onehot,
     meta_v, meta_s, table_v, table_s,
@@ -154,6 +154,9 @@
         for off in (1, 2, 3):
             part = plane.at[k, pl.ds(own, 2)]
             send(part, part, S_F1, R_F1 + k, peer(a1, off))
+        part = plane.at[k, pl.ds(own, 2)]
+        send(part, part, S_F2, R_F2 + k, peer(a2, 1))
+        send(part, part, S_F2, R_F2 + k, peer(a2, 3))
     send(x_ref.at[pl.ds(NODES - RIM, RIM)], halo.at[0], S_HALO, R_HALO, up)
     send(x_ref.at[pl.ds(0, RIM)], halo.at[1], S_HALO, R_HALO, down)
     for i, axis in enumerate(AXES):
@@ -166,8 +169,9 @@
         col = idx[:, j:j + 1].astype(jnp.int32)
         onehot[j * BLOCK:(j + 1) * BLOCK, :] = jnp.where(col == lanes, 1.0, 0.0).astype(BF)
     for k in range(COLORS):
-        for j in range(SIDE):
-            dz_all[k, j, ROWS] = jnp.zeros((BLOCK, COLS), BF)
+        for j in range(3):
+            dz_near[k, j, ROWS] = jnp.zeros((BLOCK, COLS), BF)
+        dz_far[k, ROWS] = jnp.zeros((BLOCK, COLS), BF)
     csum[...] = jnp.zeros_like(csum)
     dzown[...] = jnp.zeros_like(dzown)
     loads[0].wait()
@@ -175,9 +179,10 @@
 
     for k, (a1, a2, a3) in enumerate(ORDERS):
         arrived(plane.at[k, pl.ds(0, 6)], R_F1 + k)
-        part = plane.at[k, pl.ds(coord[a2] * 8, 8)]
-        send(part, part, S_F2, R_F2 + k, peer(a2, 1))
-        send(part, part, S_F2, R_F2 + k, peer(a2, 3))
+        for off in (1, 2, 3):
+            part = plane.at[k, pl.ds((coord[a2] * SIDE + around(a1, off)) * 2, 2)]
+            send(part, part, S_F2, R_F2 + k, peer(a2, 1))
+            send(part, part, S_F2, R_F2 + k, peer(a2, 3))
 
     arrived(halo, R_HALO)
     has_low = (me > 0).astype(F32)
@@ -347,11 +352,15 @@
             dzown[1] += part.astype(F32) * weight
             dzown[0] += part.astype(F32) * (1.0 - weight)
             for k in range(COLORS):
-                dz_all[k, 0, 2 * t + s] = part[:, k * COLS:(k + 1) * COLS]
-        for k, (a1, a2, a3) in enumerate(ORDERS):
-            pair = pl.ds(2 * t, 2)
-            send(dz_all.at[k, 0, pair], dz_all.at[k, 3, pair], S_B1, R_B1 + t, peer(a3, 1))
-            send(dz_all.at[k, 0, pair], dz_all.at[k, 1, pair], S_B1, R_B1 + t, peer(a3, 3))
+                dz_near[k, 0, 2 * t + s] = part[:, k * COLS:(k + 1) * COLS]
+
+        @pl.when(lax.rem(t, 2) == 1)
+        def _():
+            four = pl.ds(2 * t - 2, 4)
+            for k, (a1, a2, a3) in enumerate(ORDERS):
+                chunk = lax.div(t, 2)
+                send(dz_near.at[k, 0, four], dz_near.at[k, 2, four], S_B1, R_B1 + chunk, peer(a3, 1))
+                send(dz_near.at[k, 0, four], dz_near.at[k, 1, four], S_B1, R_B1 + chunk, peer(a3, 3))
 
     def put(group, row, value):
         value = value.astype(BF)
@@ -457,7 +466,7 @@
     own_low = dzown[...].reshape(NODES, L).astype(BF)
     put(CONTACT_G, 0, mm_tn(x, own_low))
     hidden = jnp.concatenate(
-        [dz_all[k, 0, 0:ROWS].reshape(ROWS * BLOCK, COLS) for k in range(COLORS)], axis=1
+        [dz_near[k, 0, 0:ROWS].reshape(ROWS * BLOCK, COLS) for k in range(COLORS)], axis=1
     )
     put(CONTACT_G, L, mm_tn(c_x[...], hidden))
     put(CONTACT_G, 2 * L, mm_tn(c_a[...], c_dy[...]))
@@ -478,12 +487,12 @@
         e_dy[rows] = dy
         e_dz[rows] = dz
 
-    def pass_on(tile):
-        arrived(dz_all.at[:, pl.ds(0, 2), pl.ds(0, 2)], R_B1 + tile)
-        for k, (a1, a2, a3) in enumerate(ORDERS):
-            even, odd = pl.ds(2 * tile, 1), pl.ds(2 * tile + 1, 1)
-            send(dz_all.at[k, 3, even], dz_all.at[k, 2, even], S_B1B, R_B1B, peer(a3, 1))
-            send(dz_all.at[k, 1, odd], dz_all.at[k, 2, odd], S_B1B, R_B1B, peer(a3, 3))
+    def pass_on(chunk):
+        arrived(dz_near.at[:, pl.ds(0, 2), pl.ds(0, 4)], R_B1 + chunk)
+        for k, (a1, a2, a3) in enumerate(ORDERS):
+            even, odd = pl.ds(4 * chunk, 2), pl.ds(4 * chunk + 2, 2)
+            send(dz_near.at[k, 2, even], dz_far.at[k, even], S_B1B, R_B1B, peer(a3, 1))
+            send(dz_near.at[k, 1, odd], dz_far.at[k, odd], S_B1B, R_B1B, peer(a3, 3))
 
     @pl.loop(0, 4)
     def _(t):
@@ -491,36 +500,48 @@
 
         @pl.when(t > 0)
         def _():
-            pass_on(2 * t - 1)
-
-        pass_on(2 * t)
+            pass_on(t - 1)
 
     write(edge_grad, edge_grad_hbm, 12)
     sums_1b(CONTACT_G)
+    sums_2(NODE_G)
     spread = mm_tn(onehot[...], e_dz[...])
     spread_low = spread.astype(BF)
     rim_out[0] = spread_low[0:RIM]
     rim_out[1] = spread_low[RIM + NODES:]
     send(rim_out.at[0], rim_in.at[0], S_RIM, R_RIM, down)
     send(rim_out.at[1], rim_in.at[1], S_RIM, R_RIM, up)
-    pass_on(7)
+    pass_on(3)
     put(EDGE_G, L, mm_tn(xext[...], spread_low))
     put(EDGE_G, 0, mm_tn(es[...], e_dz[...]))
     put(EDGE_G, 2 * L, mm_tn(x, tsum[...]))
     put(EDGE_G, 3 * L, mm_tn(e_a[...], e_dy[...]))
     sums_1(EDGE_G)
-    sums_2(NODE_G)
-
-    arrived(dz_all.at[:, 2, pl.ds(0, ROWS)], R_B1B)
+    sums_2(CONTACT_G)
+    sums_3(NODE_G)
+
     sent(plane.at[:, pl.ds(0, 16)], S_F2)
     sent(plane.at[:, pl.ds(0, 8)], S_F2B)
     sent(r3, S_F1)
 
+    @pl.loop(0, 2 * 16)
+    def _(s):
+        for k in range(COLORS):
+            total = jnp.zeros((BLOCK, COLS), F32)
+            for at, j in enumerate((0, 1, 3)):
+                for i in range(2):
+                    total += dz_near[k, at, table_s[2 * j + i, k * 32 + s]].astype(F32)
+            plane[k, s] = total.astype(BF)
+
+    sums_1b(EDGE_G)
+    sums_3(CONTACT_G)
+    sums_4(NODE_G)
+    arrived(dz_far.at[:, pl.ds(0, ROWS)], R_B1B)
+
     def slot_sum(k, s):
-        total = jnp.zeros((BLOCK, COLS), F32)
-        for j in range(SIDE):
-            for i in range(2):
-                total += dz_all[k, j, table_s[2 * j + i, k * 32 + s]].astype(F32)
+        total = plane[k, s].astype(F32)
+        for i in range(2):
+            total += dz_far[k, table_s[4 + i, k * 32 + s]].astype(F32)
         return total
 
     own, near, far, last = [[around(a2, off) * 8 for a1, a2, a3 in ORDERS] for off in range(4)]
@@ -533,8 +554,9 @@
     for k, (a1, a2, a3) in enumerate(ORDERS):
         send(plane.at[k, pl.ds(far[k], 4)], r2h.at[k, 0], S_B2H, R_B2H, peer(a2, 1))
         send(plane.at[k, pl.ds(far[k] + 4, 4)], r2h.at[k, 1], S_B2H, R_B2H, peer(a2, 3))
-    sums_1b(EDGE_G)
-    sums_2(CONTACT_G)
+    sums_2(EDGE_G)
+    sums_4(CONTACT_G)
+    sums_5(NODE_G)
 
     @pl.loop(0, 4)
     def _(s):
@@ -553,18 +575,19 @@
     for k, (a1, a2, a3) in enumerate(ORDERS):
         send(plane.at[k, pl.ds(near[k], 8)], r2.at[k, 0], S_B2, R_B2, peer(a2, 1))
         send(plane.at[k, pl.ds(last[k], 8)], r2.at[k, 1], S_B2, R_B2, peer(a2, 3))
-    sums_3(NODE_G)
+    sums_3(EDGE_G)
+    sums_5(CONTACT_G)
+    sums_6(NODE_G)
 
     @pl.loop(0, 8)
     def _(s):
         for k in range(COLORS):
             plane[k, own[k] + s] = slot_sum(k, own[k] + s).astype(BF)
 
-    sums_2(EDGE_G)
-    sums_4(NODE_G)
-    sums_3(CONTACT_G)
     grad = ncot + mm_nt(n_dz, wni[0:L]) + mm_nt(tsum[...], wei[2 * L:]) + mm_nt(own_low, wci[0:L])
 
+    sums_4(EDGE_G)
+    sums_6(CONTACT_G)
     arrived(r2, R_B2)
     for k, (a1, a2, a3) in enumerate(ORDERS):
         @pl.loop(0, 8)
@@ -579,9 +602,8 @@
                 r3src.at[k, pl.ds(around(a1, off) * 2, 2)], r3.at[k, off - 1],
                 S_B3, R_B3, peer(a1, off),
             )
-    sums_3(EDGE_G)
-    sums_5(NODE_G)
-    sums_4(CONTACT_G)
+    sums_5(EDGE_G)
+    sums_7(NODE_G)
     arrived(rim_in, R_RIM)
     first = spread[RIM:2 * RIM] + rim_in[1].astype(F32) * has_low
     last = spread[NODES:NODES + RIM] + rim_in[0].astype(F32) * has_high
@@ -597,20 +619,14 @@
     s_rem = jnp.concatenate(cols, axis=1)
     node_grad[...] = (grad + mm_nt(s_rem, wci[L:])).astype(BF)
     write(node_grad, node_grad_hbm, 13)
-
-    sums_4(EDGE_G)
-    sums_6(NODE_G)
-    sums_5(CONTACT_G)
-    sums_5(EDGE_G)
-    sums_6(CONTACT_G)
-    sums_7(NODE_G)
     sums_6(EDGE_G)
     sums_7(CONTACT_G)
     sums_7(EDGE_G)
 
+
     for ref, sem in (
         (meta_v.at[:, pl.ds(1, 3)], S_META), (halo, S_HALO), (rim_in, S_RIM), (hs, S_H), (sbuf, S_F3), (sbuf, S_B1),
-        (dz_all.at[:, 2, pl.ds(0, ROWS)], S_B1B), (r2h, S_B2H), (r2, S_B2), (r3, S_B3),
+        (dz_far.at[:, pl.ds(0, ROWS)], S_B1B), (r2h, S_B2H), (r2, S_B2), (r3, S_B3),
     ):
         sent(ref, sem)
     for n in range(3):
@@ -640,7 +656,7 @@
         [vm((COLORS, 2, CHUNK, HALF, COLS), BF) for _ in range(N_CHUNK)],
         vm((COLORS, 2, ROWS) + tile, BF),
         [vm((COLORS, 3, CHUNK) + tile, BF) for _ in range(N_CHUNK)],
-        vm((COLORS, SIDE, ROWS + 1) + tile, BF),
+        vm((COLORS, 3, ROWS + 1) + tile, BF), vm((COLORS, ROWS + 1) + tile, BF),
         vm((COLORS, 2, 4) + tile, BF), vm((COLORS, 2, 8) + tile, BF), vm((COLORS, 3, 2) + tile, BF), vm((COLORS, 8) + tile, BF),
         [vm((COLORS, rows, COLS), BF) for rows in GROUPS],
         [vm((COLORS, 2, rows // 8, COLS), BF) for rows in GROUPS],

time: 122 us -> 119 us (0.975)
  Pallas kernels: 121 us -> 118 us
    pallas_call x1, Pallas kernels: 116 us -> 113 us  [fused(): pl.pallas_call(body, out_shape=(jax.ShapeDtypeStruct((NODES, L), BF), jax...]
where the time goes in v4:
time: 119 us
  Pallas kernels  118 us (99%)
    pallas_call x1, Pallas kernels, fused(): pl.pallas_call(body, out_shape=(jax.ShapeDtypeStruct((NODES, L), BF), jax...  113 us
    pallas_call x1, Pallas kernels, finish(): pl.pallas_call(finish_body, out_shape=shapes, in_specs=[there] * 7, out_s...  4.98 us

profile of v4, /device:TPU:0, one launch (start us, length us, event | category | flops | bytes accessed | tf_op | source)
XLA Modules:
  0.0 118.8 jit_solution(744330794864333552)
XLA Ops:
  0.6 113.0 %layer.1 = (bf16[256,384]{1,0:T(8,128)(2,1)}, bf16[1024,384]{1,0:T(8,128)(2,1)}, bf16[256,384]{1,0:T(8,128)(2,1)}, bf16[1024,384]{1,0:T(8,128)(2,1)}, bf16[3,4,4...) custom-call(bf16[256,384]{1,0:T(8,128)(2,1)} %x_ref.1, ...), custom_call_target="tpu_custom_call" | custom-call | tf_op jit(solution)/shard_map/layer/pallas_call | solution.py:683
  113.7 5.0 %finish.1 = (bf16[256,384]{1,0:T(8,128)(2,1)}, bf16[1024,384]{1,0:T(8,128)(2,1)}, bf16[256,384]{1,0:T(8,128)(2,1)}, bf16[1024,384]{1,0:T(8,128)(2,1)}, f32[1152,...) custom-call(bf16[256,384]{1,0:T(8,128)(2,1)} %get-tuple-element.27.r, ...), custom_call_target="tpu_custom_call" | custom-call | tf_op jit(solution)/shard_map/finish/pallas_call | solution.py:737

commit v5 on v4

--- a/solution.py
+++ b/solution.py
@@ -459,20 +459,6 @@
 
     for k in range(COLORS):
         gsend[CONTACT_G][k, 3 * L:] = jnp.zeros((GROUPS[CONTACT_G] - 3 * L, COLS), BF)
-    put(NODE_G, 3 * L, mm_tn(a, n_dy))
-    for i in range(3):
-        put(NODE_G, i * L, mm_tn(nbuf[:, i * L:(i + 1) * L], n_dz))
-    sums_1(NODE_G)
-    own_low = dzown[...].reshape(NODES, L).astype(BF)
-    put(CONTACT_G, 0, mm_tn(x, own_low))
-    hidden = jnp.concatenate(
-        [dz_near[k, 0, 0:ROWS].reshape(ROWS * BLOCK, COLS) for k in range(COLORS)], axis=1
-    )
-    put(CONTACT_G, L, mm_tn(c_x[...], hidden))
-    put(CONTACT_G, 2 * L, mm_tn(c_a[...], c_dy[...]))
-    sums_1(CONTACT_G)
-    sums_1b(NODE_G)
-
     dmesh[...] = mm_nt(n_dz, wni[L:2 * L]).astype(BF)
     loads[7].wait()
 
@@ -494,31 +480,39 @@
             send(dz_near.at[k, 2, even], dz_far.at[k, even], S_B1B, R_B1B, peer(a3, 1))
             send(dz_near.at[k, 1, odd], dz_far.at[k, odd], S_B1B, R_B1B, peer(a3, 3))
 
-    @pl.loop(0, 4)
-    def _(t):
-        edge_backward(t)
-
-        @pl.when(t > 0)
-        def _():
-            pass_on(t - 1)
-
+    pl.loop(0, 2)(edge_backward)
+    pass_on(0)
+    pl.loop(2, 4)(edge_backward)
+    pass_on(1)
     write(edge_grad, edge_grad_hbm, 12)
-    sums_1b(CONTACT_G)
-    sums_2(NODE_G)
+    put(NODE_G, 3 * L, mm_tn(a, n_dy))
+    for i in range(3):
+        put(NODE_G, i * L, mm_tn(nbuf[:, i * L:(i + 1) * L], n_dz))
+    sums_1(NODE_G)
+    pass_on(2)
     spread = mm_tn(onehot[...], e_dz[...])
     spread_low = spread.astype(BF)
     rim_out[0] = spread_low[0:RIM]
     rim_out[1] = spread_low[RIM + NODES:]
     send(rim_out.at[0], rim_in.at[0], S_RIM, R_RIM, down)
     send(rim_out.at[1], rim_in.at[1], S_RIM, R_RIM, up)
-    pass_on(3)
     put(EDGE_G, L, mm_tn(xext[...], spread_low))
     put(EDGE_G, 0, mm_tn(es[...], e_dz[...]))
     put(EDGE_G, 2 * L, mm_tn(x, tsum[...]))
     put(EDGE_G, 3 * L, mm_tn(e_a[...], e_dy[...]))
     sums_1(EDGE_G)
-    sums_2(CONTACT_G)
-    sums_3(NODE_G)
+    sums_1b(NODE_G)
+    pass_on(3)
+    own_low = dzown[...].reshape(NODES, L).astype(BF)
+    put(CONTACT_G, 0, mm_tn(x, own_low))
+    hidden = jnp.concatenate(
+        [dz_near[k, 0, 0:ROWS].reshape(ROWS * BLOCK, COLS) for k in range(COLORS)], axis=1
+    )
+    put(CONTACT_G, L, mm_tn(c_x[...], hidden))
+    put(CONTACT_G, 2 * L, mm_tn(c_a[...], c_dy[...]))
+    sums_1(CONTACT_G)
+    sums_1b(EDGE_G)
+    sums_2(NODE_G)
 
     sent(plane.at[:, pl.ds(0, 16)], S_F2)
     sent(plane.at[:, pl.ds(0, 8)], S_F2B)
@@ -533,9 +527,9 @@
                     total += dz_near[k, at, table_s[2 * j + i, k * 32 + s]].astype(F32)
             plane[k, s] = total.astype(BF)
 
-    sums_1b(EDGE_G)
-    sums_3(CONTACT_G)
-    sums_4(NODE_G)
+    sums_1b(CONTACT_G)
+    sums_2(EDGE_G)
+    sums_3(NODE_G)
     arrived(dz_far.at[:, pl.ds(0, ROWS)], R_B1B)
 
     def slot_sum(k, s):
@@ -554,9 +548,9 @@
     for k, (a1, a2, a3) in enumerate(ORDERS):
         send(plane.at[k, pl.ds(far[k], 4)], r2h.at[k, 0], S_B2H, R_B2H, peer(a2, 1))
         send(plane.at[k, pl.ds(far[k] + 4, 4)], r2h.at[k, 1], S_B2H, R_B2H, peer(a2, 3))
-    sums_2(EDGE_G)
-    sums_4(CONTACT_G)
-    sums_5(NODE_G)
+    sums_2(CONTACT_G)
+    sums_3(EDGE_G)
+    sums_4(NODE_G)
 
     @pl.loop(0, 4)
     def _(s):
@@ -575,9 +569,9 @@
     for k, (a1, a2, a3) in enumerate(ORDERS):
         send(plane.at[k, pl.ds(near[k], 8)], r2.at[k, 0], S_B2, R_B2, peer(a2, 1))
         send(plane.at[k, pl.ds(last[k], 8)], r2.at[k, 1], S_B2, R_B2, peer(a2, 3))
-    sums_3(EDGE_G)
-    sums_5(CONTACT_G)
-    sums_6(NODE_G)
+    sums_3(CONTACT_G)
+    sums_4(EDGE_G)
+    sums_5(NODE_G)
 
     @pl.loop(0, 8)
     def _(s):
@@ -586,8 +580,9 @@
 
     grad = ncot + mm_nt(n_dz, wni[0:L]) + mm_nt(tsum[...], wei[2 * L:]) + mm_nt(own_low, wci[0:L])
 
-    sums_4(EDGE_G)
-    sums_6(CONTACT_G)
+    sums_4(CONTACT_G)
+    sums_5(EDGE_G)
+    sums_6(NODE_G)
     arrived(r2, R_B2)
     for k, (a1, a2, a3) in enumerate(ORDERS):
         @pl.loop(0, 8)
@@ -602,7 +597,8 @@
                 r3src.at[k, pl.ds(around(a1, off) * 2, 2)], r3.at[k, off - 1],
                 S_B3, R_B3, peer(a1, off),
             )
-    sums_5(EDGE_G)
+    sums_5(CONTACT_G)
+    sums_6(EDGE_G)
     sums_7(NODE_G)
     arrived(rim_in, R_RIM)
     first = spread[RIM:2 * RIM] + rim_in[1].astype(F32) * has_low
@@ -619,9 +615,9 @@
     s_rem = jnp.concatenate(cols, axis=1)
     node_grad[...] = (grad + mm_nt(s_rem, wci[L:])).astype(BF)
     write(node_grad, node_grad_hbm, 13)
-    sums_6(EDGE_G)
+    sums_6(CONTACT_G)
+    sums_7(EDGE_G)
     sums_7(CONTACT_G)
-    sums_7(EDGE_G)
 
 
     for ref, sem in (

time: 119 us -> 116 us (0.975)
  Pallas kernels: 118 us -> 115 us
    pallas_call x1, Pallas kernels: 113 us -> 110 us  [fused(): pl.pallas_call(body, out_shape=(jax.ShapeDtypeStruct((NODES, L), BF), jax...]
where the time goes in v5:
time: 116 us
  Pallas kernels  115 us (99%)
    pallas_call x1, Pallas kernels, fused(): pl.pallas_call(body, out_shape=(jax.ShapeDtypeStruct((NODES, L), BF), jax...  110 us
    pallas_call x1, Pallas kernels, finish(): pl.pallas_call(finish_body, out_shape=shapes, in_specs=[there] * 7, out_s...  4.98 us

profile of v5, /device:TPU:0, one launch (start us, length us, event | category | flops | bytes accessed | tf_op | source)
XLA Modules:
  0.0 116.1 jit_solution(218104717523236935)
XLA Ops:
  0.6 110.3 %layer.1 = (bf16[256,384]{1,0:T(8,128)(2,1)}, bf16[1024,384]{1,0:T(8,128)(2,1)}, bf16[256,384]{1,0:T(8,128)(2,1)}, bf16[1024,384]{1,0:T(8,128)(2,1)}, bf16[3,4,4...) custom-call(bf16[256,384]{1,0:T(8,128)(2,1)} %x_ref.1, ...), custom_call_target="tpu_custom_call" | custom-call | tf_op jit(solution)/shard_map/layer/pallas_call | solution.py:679
  111.0 5.0 %finish.1 = (bf16[256,384]{1,0:T(8,128)(2,1)}, bf16[1024,384]{1,0:T(8,128)(2,1)}, bf16[256,384]{1,0:T(8,128)(2,1)}, bf16[1024,384]{1,0:T(8,128)(2,1)}, f32[1152,...) custom-call(bf16[256,384]{1,0:T(8,128)(2,1)} %get-tuple-element.27.r, ...), custom_call_target="tpu_custom_call" | custom-call | tf_op jit(solution)/shard_map/finish/pallas_call | solution.py:733

commit v6 on v5

--- a/solution.py
+++ b/solution.py
@@ -71,7 +71,7 @@
 
 
 def body(
-    x_ref, src_ref, ncot_ref, block_ref, host_ref, remote_ref,
+    x_hbm, src_hbm, ncot_hbm, block_hbm, host_hbm, remote_hbm,
     es_hbm, ecot_hbm, wei_hbm, weo_hbm, wni_hbm, wno_hbm, wci_hbm, wco_hbm,
     node_out_hbm, edge_out_hbm, node_grad_hbm, edge_grad_hbm, node_hbm, contact_hbm, edge_hbm,
     es, ecot, wei, weo, wni, wno, wci, wco,
@@ -82,6 +82,7 @@
     e_u, e_r, e_h, e_a, e_dy, e_dz, mesh_sum,
     c_x, c_u, c_r, c_h, c_a, c_dy, p_own, csum, dzown, tsum, nbuf, dcon, dmesh,
     local_sem, ss, rs,
+    x_ref, src_ref, ncot_ref, block_ref, host_ref, remote_ref,
 ):
     me = lax.axis_index("dom")
     coord = {"y": lax.div(me, 16), "x": lax.rem(lax.div(me, 4), 4), "z": lax.rem(me, 4)}
@@ -109,6 +110,22 @@
     def send(*args):
         remote(*args).start()
 
+    barrier = pltpu.get_barrier_semaphore()
+    for axis in AXES:
+        for off in (1, 2, 3):
+            pl.semaphore_signal(barrier, inc=1, device_id={"dom": peer(axis, off)}, device_id_type=MESH)
+    pl.semaphore_signal(barrier, inc=1, device_id={"dom": up}, device_id_type=MESH)
+    pl.semaphore_signal(barrier, inc=1, device_id={"dom": down}, device_id_type=MESH)
+
+    early = [
+        pltpu.make_async_copy(src, dst, local_sem.at[50 + i])
+        for i, (src, dst) in enumerate(
+            [(x_hbm, x_ref), (block_hbm, block_ref), (host_hbm, host_ref), (remote_hbm, remote_ref),
+             (src_hbm, src_ref), (ncot_hbm, ncot_ref)]
+        )
+    ]
+    for load in early:
+        load.start()
     loads = [
         pltpu.make_async_copy(src, dst, local_sem.at[i])
         for i, (src, dst) in enumerate(
@@ -126,13 +143,8 @@
         out.start()
         outs.append(out)
 
-    barrier = pltpu.get_barrier_semaphore()
-    for axis in AXES:
-        for off in (1, 2, 3):
-            pl.semaphore_signal(barrier, inc=1, device_id={"dom": peer(axis, off)}, device_id_type=MESH)
-    pl.semaphore_signal(barrier, inc=1, device_id={"dom": up}, device_id_type=MESH)
-    pl.semaphore_signal(barrier, inc=1, device_id={"dom": down}, device_id_type=MESH)
-
+    for load in early[0:4]:
+        load.wait()
     x = x_ref[...]
     place = lax.broadcasted_iota(jnp.int32, (1, 128), 1)
     for c in range(ROWS):
@@ -164,6 +176,7 @@
             send(meta_v.at[i, 0], meta_v.at[i, SIDE - off], S_META, R_META, peer(axis, off))
 
     lanes = lax.broadcasted_iota(jnp.int32, (BLOCK, L), 1)
+    early[4].wait()
     idx = jnp.concatenate([src_ref[...].astype(F32)] * 16, axis=0).T
     for j in range(EDGES // BLOCK):
         col = idx[:, j:j + 1].astype(jnp.int32)
@@ -333,6 +346,7 @@
     node_out[...] = (x.astype(F32) + u).astype(BF)
     write(node_out, node_out_hbm, 10)
     write(edge_out, edge_out_hbm, 11)
+    early[5].wait()
     ncot = ncot_ref[...].astype(F32)
     n_dy = norm_back(u, r, ncot).astype(BF)
     n_dz = (mm_nt(n_dy, wno[...]) * h).astype(BF)
@@ -671,18 +685,18 @@
         vm((ROWS * BLOCK, L), BF),
         vm((ROWS * BLOCK, L), BF), vm((2, BLOCK, L), F32), vm((2, BLOCK, L), F32), vm((2, BLOCK, L), F32),
         vm((NODES, L), BF), vm((NODES, 3 * L), BF), vm((2, BLOCK, L), BF), vm((NODES, L), BF),
-        dma(50), dma(S_G + 21), dma(R_G + 21),
+        dma(56), dma(S_G + 21), dma(R_G + 21),
+        vm((NODES, L), BF), vm((8, 128), jnp.int32), vm((NODES, L), BF),
+        *[pltpu.SMEM((ROWS,), jnp.int32) for _ in range(3)],
     ]
-    here = pl.BlockSpec(memory_space=pltpu.VMEM)
     there = pl.BlockSpec(memory_space=pl.ANY)
-    scalars = pl.BlockSpec(memory_space=pltpu.SMEM)
     return pl.pallas_call(
         body,
         out_shape=(
             jax.ShapeDtypeStruct((NODES, L), BF), jax.ShapeDtypeStruct((EDGES, L), BF),
             jax.ShapeDtypeStruct((NODES, L), BF), jax.ShapeDtypeStruct((EDGES, L), BF),
         ) + tuple(jax.ShapeDtypeStruct((COLORS, SIDE, SIDE, piece, COLS), BF) for piece in pieces),
-        in_specs=[here] * 3 + [scalars] * 3 + [there] * 8,
+        in_specs=[there] * 14,
         out_specs=[there] * 7,
         scratch_shapes=scratch,
         compiler_params=pltpu.CompilerParams(

time: 116 us -> 115 us (level)
  no operation moved by 1% of the time
where the time goes in v6:
time: 115 us
  Pallas kernels  114 us (99%)
    pallas_call x1, Pallas kernels, fused(): pl.pallas_call(body, out_shape=(jax.ShapeDtypeStruct((NODES, L), BF), jax...  109 us
    pallas_call x1, Pallas kernels, finish(): pl.pallas_call(finish_body, out_shape=shapes, in_specs=[there] * 7, out_s...  4.98 us

profile of v6, /device:TPU:0, one launch (start us, length us, event | category | flops | bytes accessed | tf_op | source)
XLA Modules:
  0.0 115.1 jit_solution(3439694149192161948)
XLA Ops:
  0.6 109.3 %layer.1 = (bf16[256,384]{1,0:T(8,128)(2,1)}, bf16[1024,384]{1,0:T(8,128)(2,1)}, bf16[256,384]{1,0:T(8,128)(2,1)}, bf16[1024,384]{1,0:T(8,128)(2,1)}, bf16[3,4,4...) custom-call(bf16[256,384]{1,0:T(8,128)(2,1)} %x_hbm.1, ...), custom_call_target="tpu_custom_call" | custom-call | tf_op jit(solution)/shard_map/layer/pallas_call | solution.py:693
  109.9 5.0 %finish.1 = (bf16[256,384]{1,0:T(8,128)(2,1)}, bf16[1024,384]{1,0:T(8,128)(2,1)}, bf16[256,384]{1,0:T(8,128)(2,1)}, bf16[1024,384]{1,0:T(8,128)(2,1)}, f32[1152,...) custom-call(bf16[256,384]{1,0:T(8,128)(2,1)} %get-tuple-element.27.r, ...), custom_call_target="tpu_custom_call" | custom-call | tf_op jit(solution)/shard_map/finish/pallas_call | solution.py:747
